TPU v7x, 32 devices: a whole 2x2x4 slice. The times are simulated.
32 devices in a mesh: ctx: 8 (over z, y), fsdp: 4 (over x, core).
Axes of the slice: x: 2, y: 2, z: 4, core: 2. Of those that a mesh axis runs over, the one named last changes fastest.
Arguments:
- tokens: bfloat16 [4, 16, 128, 1024], P('fsdp', None, 'ctx'), may hold values from -6 to 6
- lengths: int32 [4, 3], P('fsdp'), may hold values from 512 to 1024, as said below
- packing: int32 [4, 3], P('fsdp'), may hold values from 0 to 2, each once within a row
- query_w: bfloat16 [1024, 1024], P('fsdp'), may hold values from -0.1875 to 0.1875
- query_b: float32 [1024], replicated, may hold values from -3 to 3
- key_w: bfloat16 [1024, 1024], P('fsdp'), may hold values from -0.1875 to 0.1875
- value_w: bfloat16 [1024, 1024], P('fsdp'), may hold values from -0.1875 to 0.1875
- value_b: float32 [1024], replicated, may hold values from -3 to 3
- output_w: bfloat16 [1024, 1024], P('fsdp'), may hold values from -3 to 3
- output_b: float32 [1024], replicated, may hold values from -3 to 3
- attn_gain: float32 [1024], replicated, may hold values from 0.5 to 1.5
- attn_shift: float32 [1024], replicated, may hold values from -2 to 2
- expand_w: bfloat16 [1024, 4096], P('fsdp'), may hold values from -0.1875 to 0.1875
- expand_b: float32 [4096], replicated, may hold values from -3 to 3
- reduce_w: bfloat16 [4096, 1024], P('fsdp'), may hold values from -0.09375 to 0.09375
- reduce_b: float32 [1024], replicated, may hold values from -3 to 3
- ffn_gain: float32 [1024], replicated, may hold values from 0.5 to 1.5
- ffn_shift: float32 [1024], replicated, may hold values from -2 to 2
- cotangent: bfloat16 [4, 16, 128, 1024], P('fsdp', None, 'ctx'), may hold values from -6 to 6
Outputs:
- layer_out: bfloat16 [4, 16, 128, 1024], P('fsdp', None, 'ctx')
- grad_tokens: float32 [4, 16, 128, 1024], P('fsdp', None, 'ctx')
- grad_query_w: float32 [1024, 1024], P('fsdp')
- grad_query_b: float32 [1024], replicated
- grad_key_w: float32 [1024, 1024], P('fsdp')
- grad_value_w: float32 [1024, 1024], P('fsdp')
- grad_value_b: float32 [1024], replicated
- grad_output_w: float32 [1024, 1024], P('fsdp')
- grad_output_b: float32 [1024], replicated
- grad_attn_gain: float32 [1024], replicated
- grad_attn_shift: float32 [1024], replicated
- grad_expand_w: float32 [1024, 4096], P('fsdp')
- grad_expand_b: float32 [4096], replicated
- grad_reduce_w: float32 [4096, 1024], P('fsdp')
- grad_reduce_b: float32 [1024], replicated
- grad_ffn_gain: float32 [1024], replicated
- grad_ffn_shift: float32 [1024], replicated
Inputs may be any that keep to these rules, and one draw needn't show every extreme that they name: Each row's 3 lengths sum to 2048. Each row of packing names every sequence once.
All inputs are finite; a program needn't handle non-finite values.
Results may differ from a plain program's by a relative error of at most 0.02.
Values may be sent and summed in bfloat16 or wider, within the bound.
A program may use at most 192 MiB of HBM per device.

v0:
```python
import jax
import jax.numpy as jnp
from jax import lax
from jax.sharding import PartitionSpec as P

H = 16
HD = 64


def from_behind(block, axis, distance):
    devices = range(lax.axis_size(axis))
    route = [((i - distance) % len(devices), i) for i in devices]
    return lax.ppermute(block, axis, route)


def dense(left, right):
    return jnp.dot(left, right, preferred_element_type=jnp.float32)


def dense_back(left, right):
    return lax.dot_general(
        left, right, (((1,), (1,)), ((), ())), preferred_element_type=jnp.float32
    )


def norm_fwd(hidden, gain, shift):
    mean_row = jnp.mean(hidden, axis=-1, keepdims=True)
    centred = hidden - mean_row
    variance = jnp.mean(centred * centred, axis=-1, keepdims=True)
    inv_std = lax.rsqrt(variance + 1e-05)
    x_hat = centred * inv_std
    return (x_hat * gain + shift, x_hat, inv_std)


def norm_back(incoming, x_hat, inv_std, gain):
    scaled = incoming * gain
    grad_in = inv_std * (
        scaled
        - jnp.mean(scaled, axis=-1, keepdims=True)
        - x_hat * jnp.mean(scaled * x_hat, axis=-1, keepdims=True)
    )
    return (grad_in, jnp.sum(incoming * x_hat, axis=0), jnp.sum(incoming, axis=0))


def gelu_slope(pre_act):
    return (
        0.5 * (1.0 + lax.erf(pre_act * 0.7071067811865476))
        + pre_act * jnp.exp(-0.5 * pre_act * pre_act) * 0.3989422804014327
    )


def online_update(running, query_heads, query_seg, key_rows, value_rows, key_seg):
    accum, run_max, run_sum = running
    rows_here = key_rows.shape[0]
    scores = 0.125 * jnp.einsum(
        "qhd,khd->hqk",
        query_heads,
        key_rows.reshape(rows_here, H, HD),
        preferred_element_type=jnp.float32,
    )
    same_seg = (query_seg[:, None] == key_seg[None, :])[None]
    masked = jnp.where(same_seg, scores, -1e30)
    new_max = jnp.maximum(run_max, jnp.max(masked, axis=-1))
    scale_old = jnp.exp(run_max - new_max)
    exp_scores = jnp.where(same_seg, jnp.exp(masked - new_max[:, :, None]), 0.0)
    run_sum = run_sum * scale_old + jnp.sum(exp_scores, axis=-1)
    update = jnp.einsum(
        "hqk,khd->qhd",
        exp_scores.astype(jnp.bfloat16),
        value_rows.reshape(rows_here, H, HD),
        preferred_element_type=jnp.float32,
    )
    accum = accum * scale_old.T[:, :, None] + update
    return (accum, new_max, run_sum)


def pair_grads(query_rows, grad_rows, log_sum, delta_row, query_seg, key_rows, value_rows, key_seg):
    q_heads = query_rows.reshape(-1, H, HD)
    g_heads = grad_rows.reshape(-1, H, HD)
    k_heads = key_rows.reshape(-1, H, HD)
    v_heads = value_rows.reshape(-1, H, HD)
    scores = 0.125 * jnp.einsum(
        "qhd,khd->hqk", q_heads, k_heads, preferred_element_type=jnp.float32
    )
    same_seg = (query_seg[:, None] == key_seg[None, :])[None]
    probs = jnp.where(
        same_seg, jnp.exp(jnp.where(same_seg, scores, -1e30) - log_sum[:, :, None]), 0.0
    )
    grad_prob = jnp.einsum("qhd,khd->hqk", g_heads, v_heads, preferred_element_type=jnp.float32)
    grad_score = (probs * (grad_prob - delta_row[:, :, None])).astype(jnp.bfloat16)
    grad_q = 0.125 * jnp.einsum(
        "hqk,khd->qhd", grad_score, k_heads, preferred_element_type=jnp.float32
    )
    grad_k = 0.125 * jnp.einsum(
        "hqk,qhd->khd", grad_score, q_heads, preferred_element_type=jnp.float32
    )
    grad_v = jnp.einsum(
        "hqk,qhd->khd", probs.astype(jnp.bfloat16), g_heads, preferred_element_type=jnp.float32
    )
    return (
        grad_q.reshape(query_rows.shape),
        grad_k.reshape(key_rows.shape),
        grad_v.reshape(key_rows.shape),
    )


def owner_rows(layer_in, layer_grad):
    return lax.psum_scatter(
        lax.dot_general(
            layer_in, layer_grad, (((0,), (0,)), ((), ())), preferred_element_type=jnp.float32
        ).astype(jnp.bfloat16),
        "fsdp",
        scatter_dimension=0,
        tiled=True,
    ).astype(jnp.float32)


def body(
    tokens,
    lengths,
    packing,
    query_w,
    query_b,
    key_w,
    value_w,
    value_b,
    output_w,
    output_b,
    attn_gain,
    attn_shift,
    expand_w,
    expand_b,
    reduce_w,
    reduce_b,
    ffn_gain,
    ffn_shift,
    cotangent,
):
    tok_shape = tokens.shape
    stripe = tok_shape[2]
    block_len = tok_shape[1] * tok_shape[2]
    model_width = tok_shape[3]
    n_ctx = lax.axis_size("ctx")
    ctx_index = lax.axis_index("ctx")
    seq_lens = lengths[0]
    slot_ids = packing[0]
    ordered = jnp.sum(
        jnp.where(
            slot_ids[:, None] == jnp.arange(seq_lens.shape[0], dtype=jnp.int32)[None, :],
            seq_lens[None, :],
            0,
        ),
        axis=1,
    )
    slots = jnp.arange(seq_lens.shape[0], dtype=jnp.int32)
    slot_ends = jnp.sum(jnp.where(slots[None, :] <= slots[:, None], ordered[None, :], 0), axis=1)
    gathered = jnp.arange(n_ctx * block_len, dtype=jnp.int32)
    owner_dev = gathered // block_len
    local_row = gathered % block_len
    position = local_row // stripe * (stripe * n_ctx) + owner_dev * stripe + local_row % stripe
    seg_all = jnp.sum((position[:, None] >= slot_ends[None, :]).astype(jnp.int32), axis=1)
    query_seg = lax.dynamic_slice_in_dim(seg_all, ctx_index * block_len, block_len)
    inputs = tokens.reshape(block_len, model_width)
    w_query, w_key, w_value, w_output, w_up, w_down = (
        lax.all_gather(query_w, "fsdp", axis=0, tiled=True),
        lax.all_gather(key_w, "fsdp", axis=0, tiled=True),
        lax.all_gather(value_w, "fsdp", axis=0, tiled=True),
        lax.all_gather(output_w, "fsdp", axis=0, tiled=True),
        lax.all_gather(expand_w, "fsdp", axis=0, tiled=True),
        lax.all_gather(reduce_w, "fsdp", axis=0, tiled=True),
    )
    queries = (dense(inputs, w_query) + query_b).astype(jnp.bfloat16)
    key_rows = dense(inputs, w_key).astype(jnp.bfloat16)
    values = (dense(inputs, w_value) + value_b).astype(jnp.bfloat16)
    query_heads = queries.reshape(block_len, H, HD)
    start_state = (
        jnp.zeros((block_len, H, HD), jnp.float32),
        jnp.full((H, block_len), -1e30, jnp.float32),
        jnp.zeros((H, block_len), jnp.float32),
    )
    key_piece = lax.all_gather(key_rows, "ctx", axis=0, tiled=True)
    value_piece = lax.all_gather(values, "ctx", axis=0, tiled=True)
    shards = key_piece.shape[0] // block_len

    def one_shard(index, inner):
        key_part = lax.dynamic_slice_in_dim(key_piece, index * block_len, block_len)
        value_part = lax.dynamic_slice_in_dim(value_piece, index * block_len, block_len)
        key_seg = lax.dynamic_slice_in_dim(seg_all, index * block_len, block_len)
        return online_update(inner, query_heads, query_seg, key_part, value_part, key_seg)

    accum, run_max, run_sum = lax.fori_loop(0, shards, one_shard, start_state)
    attended = (accum / run_sum.T[:, :, None]).reshape(block_len, model_width).astype(jnp.bfloat16)
    log_sum = run_max + jnp.log(run_sum)
    branch = dense(attended, w_output) + output_b
    normed, x_hat1, inv_std1 = norm_fwd(inputs.astype(jnp.float32) + branch, attn_gain, attn_shift)
    normed_low = normed.astype(jnp.bfloat16)
    pre_act = dense(normed_low, w_up) + expand_b
    hidden = jax.nn.gelu(pre_act, approximate=False).astype(jnp.bfloat16)
    ffn_out = dense(hidden, w_down) + reduce_b
    outputs, x_hat2, inv_std2 = norm_fwd(normed + ffn_out, ffn_gain, ffn_shift)
    layer_out = outputs.astype(jnp.bfloat16).reshape(tok_shape)
    upstream = cotangent.reshape(block_len, model_width).astype(jnp.float32)
    grad_mid2, grad_ffn_gain, grad_ffn_shift = norm_back(upstream, x_hat2, inv_std2, ffn_gain)
    grad_ffn = grad_mid2.astype(jnp.bfloat16)
    grad_reduce_b = jnp.sum(grad_ffn.astype(jnp.float32), axis=0)
    share_down = owner_rows(hidden, grad_ffn)
    grad_pre = (dense_back(grad_ffn, w_down) * gelu_slope(pre_act)).astype(jnp.bfloat16)
    grad_expand_b = jnp.sum(grad_pre.astype(jnp.float32), axis=0)
    share_up = owner_rows(normed_low, grad_pre)
    grad_normed = dense_back(grad_pre, w_up) + grad_mid2
    grad_mid1, grad_attn_gain, grad_attn_shift = norm_back(grad_normed, x_hat1, inv_std1, attn_gain)
    grad_branch = grad_mid1.astype(jnp.bfloat16)
    grad_output_b = jnp.sum(grad_branch.astype(jnp.float32), axis=0)
    share_out = owner_rows(attended, grad_branch)
    grad_att = dense_back(grad_branch, w_output).astype(jnp.bfloat16)
    delta_row = jnp.einsum(
        "qhd,qhd->hq",
        grad_att.astype(jnp.float32).reshape(block_len, H, HD),
        attended.astype(jnp.float32).reshape(block_len, H, HD),
    )
    zero_rows = jnp.zeros((block_len, model_width), jnp.float32)

    def key_step(step, state):
        visit_keys, visit_values, sum_k, sum_v, sum_q = state
        anchor = (ctx_index - step) % n_ctx
        key_seg = lax.dynamic_slice_in_dim(seg_all, anchor * block_len, block_len)
        part_q, part_k, part_v = pair_grads(
            queries, grad_att, log_sum, delta_row, query_seg, visit_keys, visit_values, key_seg
        )
        sum_q = sum_q + part_q
        visit_keys, visit_values = from_behind((visit_keys, visit_values), "ctx", 1)
        sum_k, sum_v = (
            from_behind((sum_k + part_k).astype(jnp.bfloat16), "ctx", 1).astype(jnp.float32),
            from_behind((sum_v + part_v).astype(jnp.bfloat16), "ctx", 1).astype(jnp.float32),
        )
        return (visit_keys, visit_values, sum_k, sum_v, sum_q)

    final = lax.fori_loop(0, n_ctx, key_step, (key_rows, values, zero_rows, zero_rows, zero_rows))
    sum_k, sum_v, sum_q = (final[2], final[3], final[4])
    grad_q = sum_q.astype(jnp.bfloat16)
    grad_k = sum_k.astype(jnp.bfloat16)
    grad_v = sum_v.astype(jnp.bfloat16)
    grad_query_b = jnp.sum(grad_q.astype(jnp.float32), axis=0)
    grad_value_b = jnp.sum(grad_v.astype(jnp.float32), axis=0)
    share_query = owner_rows(inputs, grad_q)
    share_key = owner_rows(inputs, grad_k)
    share_value = owner_rows(inputs, grad_v)
    grad_inputs = (
        dense_back(grad_q, w_query)
        + dense_back(grad_k, w_key)
        + dense_back(grad_v, w_value)
        + grad_mid1
    )
    share_query, share_key, share_value, share_out, share_up, share_down = lax.psum(
        (share_query, share_key, share_value, share_out, share_up, share_down), "ctx"
    )
    (
        grad_query_b,
        grad_value_b,
        grad_output_b,
        grad_attn_gain,
        grad_attn_shift,
        grad_expand_b,
        grad_reduce_b,
        grad_ffn_gain,
        grad_ffn_shift,
    ) = lax.psum(
        (
            grad_query_b,
            grad_value_b,
            grad_output_b,
            grad_attn_gain,
            grad_attn_shift,
            grad_expand_b,
            grad_reduce_b,
            grad_ffn_gain,
            grad_ffn_shift,
        ),
        ("ctx", "fsdp"),
    )
    return (
        layer_out,
        grad_inputs.reshape(tok_shape),
        share_query,
        grad_query_b,
        share_key,
        share_value,
        grad_value_b,
        share_out,
        grad_output_b,
        grad_attn_gain,
        grad_attn_shift,
        share_up,
        grad_expand_b,
        share_down,
        grad_reduce_b,
        grad_ffn_gain,
        grad_ffn_shift,
    )


def solution(mesh):
    return jax.shard_map(
        body,
        mesh=mesh,
        in_specs=(
            P("fsdp", None, "ctx", None),
            P("fsdp", None),
            P("fsdp", None),
            P("fsdp", None),
            P(),
            P("fsdp", None),
            P("fsdp", None),
            P(),
            P("fsdp", None),
            P(),
            P(),
            P(),
            P("fsdp", None),
            P(),
            P("fsdp", None),
            P(),
            P(),
            P(),
            P("fsdp", None, "ctx", None),
        ),
        out_specs=(
            P("fsdp", None, "ctx", None),
            P("fsdp", None, "ctx", None),
            P("fsdp", None),
            P(),
            P("fsdp", None),
            P("fsdp", None),
            P(),
            P("fsdp", None),
            P(),
            P(),
            P(),
            P("fsdp", None),
            P(),
            P("fsdp", None),
            P(),
            P(),
            P(),
        ),
        check_vma=False,
    )
```

profile of v0, /device:TPU:0, one launch (start us, length us, event | category | flops | bytes accessed | tf_op | source)
XLA Modules:
  0.0 1579.9 jit_solution(7767871707761352350)
XLA Ops:
  9.5 25.4 %all-gather.9.cloned.1.call-done = bf16[1024,1024]{1,0:T(8,128)(2,1)} async-done(((bf16[256,1024]{1,0:T(8,128)(2,1)}), bf16[1024,1024]{1,0:T(8,128)(2,1)}) %all-gather.9.cloned.1.call-update) | async-done | bytes 2097168 | tf_op jit(solution)/shard_map/all_gather | solution.py:166
  34.9 3.3 convolution_convert_fusion.4
  38.3 20.8 %all-gather.15.cloned.1.call-done = bf16[1024,1024]{1,0:T(8,128)(2,1)} async-done(((bf16[256,1024]{1,0:T(8,128)(2,1)}), bf16[1024,1024]{1,0:T(8,128)(2,1)}) %all-gather.15.cloned.1.call-update) | async-done | bytes 2097168 | tf_op jit(solution)/shard_map/all_gather | solution.py:167
  59.1 3.1 fusion.45
  67.9 15.4 all-gather.13.cloned.1.call-done
  85.8 73.5 %all-gather.11.cloned.1.call-done = bf16[2048,1024]{1,0:T(8,128)(2,1)} async-done(((bf16[256,1024]{1,0:T(8,128)(2,1)}), bf16[2048,1024]{1,0:T(8,128)(2,1)}) %all-gather.11.cloned.1.call-update) | async-done | bytes 4194320 | tf_op jit(solution)/shard_map/all_gather | solution.py:181
  159.3 74.2 %all-gather.17.cloned.1.call-done = bf16[2048,1024]{1,0:T(8,128)(2,1)} async-done(((bf16[256,1024]{1,0:T(8,128)(2,1)}), bf16[2048,1024]{1,0:T(8,128)(2,1)}) %all-gather.17.cloned.1.call-update) | async-done | bytes 4194320 | tf_op jit(solution)/shard_map/all_gather | solution.py:182
  233.6 103.5 %while.42 = (s32[]{:T(128)}, f32[256,16,64]{0,2,1:T(8,128)}, f32[16,256]{1,0:T(8,128)S(1)}, f32[16,256]{1,0:T(8,128)S(1)}, s32[256]{0:T(256)S(1)}, /*index=5*/s3...) while((s32[]{:T(128)}, f32[256,16,64]{0,2,1:T(8,128)}, ...), condition=%wide.region_6.7_spmd.clone, body=%wide.region_3.6_spmd.clone.sunk | while | flops 282943488 | bytes 20975804 | solution.py:191
  238.1 3.4 fusion.156
  241.8 4.3 fusion.155
  250.6 3.2 fusion.156
  254.1 4.6 fusion.155
  263.2 3.8 fusion.156
  267.2 5.8 fusion.155
  277.6 3.2 fusion.156
  281.0 4.7 fusion.155
  290.2 3.2 fusion.156
  293.6 4.6 fusion.155
  302.8 3.3 fusion.156
  306.3 4.6 fusion.155
  315.4 3.2 fusion.156
  318.8 4.6 fusion.155
  325.3 3.1 fusion.153
  328.4 3.9 fusion.156
  332.5 4.6 fusion.155
  341.5 15.8 fusion.29
  357.3 18.4 %all-gather.23.cloned.1.call-done = bf16[4096,1024]{1,0:T(8,128)(2,1)} async-done(((bf16[1024,1024]{1,0:T(8,128)(2,1)}), bf16[4096,1024]{1,0:T(8,128)(2,1)}) %all-gather.23.cloned.1.call-update) | async-done | bytes 8388624 | tf_op jit(solution)/shard_map/all_gather | solution.py:170
  375.6 6.6 fusion.88
  384.5 4.2 convert_reduce_fusion
  394.0 406.6 %while.43 = (s32[]{:T(128)}, bf16[256,1024]{0,1:T(8,128)(2,1)}, bf16[256,1024]{0,1:T(8,128)(2,1)}, f32[256,1024]{0,1:T(8,128)}, f32[256,1024]{0,1:T(8,128)}, /*i...) while((s32[]{:T(128)}, bf16[256,1024]{0,1:T(8,128)(2,1)}, ...), condition=%wide.region_16.17_spmd.clone, body=%wide.region_15.16_spmd.clone.sunk | while | flops 686882816 | bytes 68932264 | solution.py:238
  401.2 3.1 multiply_convert_fusion.2
  414.1 21.3 %collective-permute-done.2 = bf16[256,1024]{0,1:T(8,128)(2,1)} collective-permute-done((bf16[256,1024]{0,1:T(8,128)(2,1)}, bf16[256,1024]{0,1:T(8,128)(2,1)}, u32[]{:S(2)}, u32[]{:S(2)}) %collective-permute-start.2) | collective-permute-done | bytes 524320 | tf_op jit(solution)/shard_map/while/body/eval_jaxpr/ppermute | solution.py:13
  437.5 8.5 collective-permute-done.3
  453.3 3.1 multiply_convert_fusion.2
  466.3 23.2 %collective-permute-done.2 = bf16[256,1024]{0,1:T(8,128)(2,1)} collective-permute-done((bf16[256,1024]{0,1:T(8,128)(2,1)}, bf16[256,1024]{0,1:T(8,128)(2,1)}, u32[]{:S(2)}, u32[]{:S(2)}) %collective-permute-start.2) | collective-permute-done | bytes 524320 | tf_op jit(solution)/shard_map/while/body/eval_jaxpr/ppermute | solution.py:13
  491.6 7.5 collective-permute-done.3
  505.3 3.1 multiply_convert_fusion.2
  517.6 25.0 %collective-permute-done.2 = bf16[256,1024]{0,1:T(8,128)(2,1)} collective-permute-done((bf16[256,1024]{0,1:T(8,128)(2,1)}, bf16[256,1024]{0,1:T(8,128)(2,1)}, u32[]{:S(2)}, u32[]{:S(2)}) %collective-permute-start.2) | collective-permute-done | bytes 524320 | tf_op jit(solution)/shard_map/while/body/eval_jaxpr/ppermute | solution.py:13
  544.7 6.6 collective-permute-done.3
  557.5 3.1 multiply_convert_fusion.2
  568.0 26.8 %collective-permute-done.2 = bf16[256,1024]{0,1:T(8,128)(2,1)} collective-permute-done((bf16[256,1024]{0,1:T(8,128)(2,1)}, bf16[256,1024]{0,1:T(8,128)(2,1)}, u32[]{:S(2)}, u32[]{:S(2)}) %collective-permute-start.2) | collective-permute-done | bytes 524320 | tf_op jit(solution)/shard_map/while/body/eval_jaxpr/ppermute | solution.py:13
  596.9 5.7 collective-permute-done.3
  608.8 3.1 multiply_convert_fusion.2
  618.9 27.2 %collective-permute-done.2 = bf16[256,1024]{0,1:T(8,128)(2,1)} collective-permute-done((bf16[256,1024]{0,1:T(8,128)(2,1)}, bf16[256,1024]{0,1:T(8,128)(2,1)}, u32[]{:S(2)}, u32[]{:S(2)}) %collective-permute-start.2) | collective-permute-done | bytes 524320 | tf_op jit(solution)/shard_map/while/body/eval_jaxpr/ppermute | solution.py:13
  648.2 4.8 collective-permute-done.3
  659.1 3.1 multiply_convert_fusion.2
  669.2 27.2 %collective-permute-done.2 = bf16[256,1024]{0,1:T(8,128)(2,1)} collective-permute-done((bf16[256,1024]{0,1:T(8,128)(2,1)}, bf16[256,1024]{0,1:T(8,128)(2,1)}, u32[]{:S(2)}, u32[]{:S(2)}) %collective-permute-start.2) | collective-permute-done | bytes 524320 | tf_op jit(solution)/shard_map/while/body/eval_jaxpr/ppermute | solution.py:13
  698.5 3.8 collective-permute-done.3
  708.6 3.1 multiply_convert_fusion.2
  718.6 26.6 %collective-permute-done.2 = bf16[256,1024]{0,1:T(8,128)(2,1)} collective-permute-done((bf16[256,1024]{0,1:T(8,128)(2,1)}, bf16[256,1024]{0,1:T(8,128)(2,1)}, u32[]{:S(2)}, u32[]{:S(2)}) %collective-permute-start.2) | collective-permute-done | bytes 524320 | tf_op jit(solution)/shard_map/while/body/eval_jaxpr/ppermute | solution.py:13
  747.3 3.5 collective-permute-done.3
  757.1 3.1 multiply_convert_fusion.2
  767.1 25.7 %collective-permute-done.2 = bf16[256,1024]{0,1:T(8,128)(2,1)} collective-permute-done((bf16[256,1024]{0,1:T(8,128)(2,1)}, bf16[256,1024]{0,1:T(8,128)(2,1)}, u32[]{:S(2)}, u32[]{:S(2)}) %collective-permute-start.2) | collective-permute-done | bytes 524320 | tf_op jit(solution)/shard_map/while/body/eval_jaxpr/ppermute | solution.py:13
  794.9 3.5 collective-permute-done.3
  800.6 3.5 convert_bitcast_fusion.2
  808.5 3.6 convolution_convert_fusion.2
  812.2 7.3 convolution_convert_fusion.1
  820.8 7.2 convolution_convert_fusion
  829.4 38.5 %all-reduce = (f32[1024]{0:T(1024)}, f32[1024]{0:T(1024)}, f32[1024]{0:T(1024)}, f32[1024]{0:T(1024)}, f32[1024]{0:T(1024)}, /*index=5*/f32[4096]{0:T(1024)}, f32[1024]{0:T(1024)}, f32[1024]{0:T(1024)}, f32[1024]{0:T(1024)}) all-reduce(f32[1024]{0:T(1024)S(1)} %convert_reduce_fusion.5, ...), channel_id=1, replica_groups=mesh['ctx'=8,'fsdp'=4] {'ctx','fsdp'}, use_global_device_ids=true, to_apply=%region_20.21 | all-reduce | flops 12288 | bytes 98304 | tf_op jit(solution)/shard_map/psum | solution.py:267
  874.6 26.8 %reduce-scatter.11.cloned.1.call-done = bf16[256,1024]{0,1:T(8,128)(2,1)} async-done(((bf16[1024,1024]{0,1:T(8,128)(2,1)}), bf16[256,1024]{0,1:T(8,128)(2,1)}) %reduce-scatter.11.cloned.1.call-update) | async-done | bytes 524304 | tf_op jit(solution)/shard_map/reduce_scatter | solution.py:108
  901.4 34.0 %reduce-scatter.13.cloned.1.call-done = bf16[256,1024]{1,0:T(8,128)(2,1)} async-done(((bf16[1024,1024]{1,0:T(8,128)(2,1)}), bf16[256,1024]{1,0:T(8,128)(2,1)}) %reduce-scatter.13.cloned.1.call-update) | async-done | bytes 524304 | tf_op jit(solution)/shard_map/reduce_scatter | solution.py:108
  935.4 74.3 %reduce-scatter.15.cloned.1.call-done = bf16[256,4096]{1,0:T(8,128)(2,1)} async-done(((bf16[1024,4096]{1,0:T(8,128)(2,1)}), bf16[256,4096]{1,0:T(8,128)(2,1)}) %reduce-scatter.15.cloned.1.call-update) | async-done | bytes 2097168 | tf_op jit(solution)/shard_map/reduce_scatter | solution.py:108
  1009.7 74.4 %reduce-scatter.17.cloned.1.call-done = bf16[1024,1024]{1,0:T(8,128)(2,1)} async-done(((bf16[4096,1024]{1,0:T(8,128)(2,1)}), bf16[1024,1024]{1,0:T(8,128)(2,1)}) %reduce-scatter.17.cloned.1.call-update) | async-done | bytes 2097168 | tf_op jit(solution)/shard_map/reduce_scatter | solution.py:108
  1084.1 485.2 %all-reduce.3 = (f32[256,1024]{0,1:T(8,128)S(1)}, f32[256,1024]{0,1:T(8,128)S(1)}, f32[256,1024]{0,1:T(8,128)S(1)}, f32[256,1024]{1,0:T(8,128)}, f32[256,4096]{1,0:T(8,128)}, /*index=5*/f32[1024,1024]{1,0:T(8,128)}) all-reduce(bf16[256,1024]{0,1:T(8,128)(2,1)} %reduce-scatter.7.cloned.1.call-done, ...), channel_id=1, replica_groups=mesh['ctx'=8,'fsdp'=4] {'ctx'}, use_global_device_ids=true, to_apply=%region_18.19 | all-reduce | flops 3145728 | bytes 18874368 | tf_op jit(solution)/shard_map/psum | solution.py:254
  (471 shorter events, 208.3 us)
Async XLA Ops:
  7.2 51.9 %copy-start.11 = (bf16[1,16,16,1024]{3,2,1,0:T(8,128)(2,1)S(1)}, bf16[1,16,16,1024]{3,2,1,0:T(8,128)(2,1)}, u32[]{:S(2)}) copy-start(bf16[1,16,16,1024]{3,2,1,0:T(8,128)(2,1)} %param.23) | copy-start | bytes 1572868
  7.2 51.9 %copy-start.32 = (f32[1024]{0:T(1024)S(1)}, f32[1024]{0:T(1024)}, u32[]{:S(2)}) copy-start(f32[1024]{0:T(1024)} %param.30) | copy-start | bytes 12292
  7.2 27.7 %all-gather.9.cloned.1.call-start = ((), (), s32[]{:S(2)}) async-start(), calls=%async_computation.6 | async-start | bytes 2621440 | tf_op jit(solution)/shard_map/all_gather | solution.py:166
  7.9 51.2 %all-gather.15.cloned.1.call-start = ((), (), s32[]{:S(2)}) async-start(), calls=%async_computation.9 | async-start | bytes 2621440 | tf_op jit(solution)/shard_map/all_gather | solution.py:167
  8.7 74.6 %all-gather.13.cloned.1.call-start = ((), (), s32[]{:S(2)}) async-start(), calls=%async_computation.8 | async-start | bytes 2621440 | tf_op jit(solution)/shard_map/all_gather | solution.py:165
  9.4 149.9 %all-gather.11.cloned.1.call-start = ((), (), s32[]{:S(2)}) async-start(), calls=%async_computation.7 | async-start | bytes 4718592 | tf_op jit(solution)/shard_map/all_gather | solution.py:181
  38.3 195.3 %all-gather.17.cloned.1.call-start = ((), (), s32[]{:S(2)}) async-start(), calls=%async_computation.10 | async-start | bytes 4718592 | tf_op jit(solution)/shard_map/all_gather | solution.py:182
  62.2 276.3 %all-gather.19.cloned.1.call-start = ((), (), s32[]{:S(2)}) async-start(), calls=%async_computation.11 | async-start | bytes 2621440 | tf_op jit(solution)/shard_map/all_gather | solution.py:168
  62.8 278.6 %all-gather.21.cloned.1.call-start = ((), (), s32[]{:S(2)}) async-start(), calls=%async_computation.12 | async-start | bytes 10485760 | tf_op jit(solution)/shard_map/all_gather | solution.py:169
  63.6 312.1 %all-gather.23.cloned.1.call-start = ((), (), s32[]{:S(2)}) async-start(), calls=%async_computation.13 | async-start | bytes 10485760 | tf_op jit(solution)/shard_map/all_gather | solution.py:170
  64.3 810.3 %reduce-scatter.7.cloned.1.call-start = ((), (), s32[]{:S(2)}) async-start(), calls=%async_computation.14 | async-start | bytes 2621440 | tf_op jit(solution)/shard_map/reduce_scatter | solution.py:108
  233.6 105.0 %copy-start.28 = (f32[1024]{0:T(1024)S(1)}, f32[1024]{0:T(1024)}, u32[]{:S(2)}) copy-start(f32[1024]{0:T(1024)} %param.32) | copy-start | bytes 12292
  341.1 50.3 %copy-start.7 = (f32[256,1024]{1,0:T(8,128)}, f32[256,1024]{1,0:T(8,128)S(1)}, u32[]{:S(2)}) copy-start(f32[256,1024]{1,0:T(8,128)S(1)} %get-tuple-element.758) | copy-start | bytes 3145732
  341.4 34.2 %copy-start.34 = (f32[1024]{0:T(1024)S(1)}, f32[1024]{0:T(1024)}, u32[]{:S(2)}) copy-start(f32[1024]{0:T(1024)} %param.38) | copy-start | bytes 12292
  395.4 52.7 %collective-permute-start = (bf16[256,1024]{0,1:T(8,128)(2,1)S(1)}, bf16[256,1024]{0,1:T(8,128)(2,1)}, u32[]{:S(2)}, u32[]{:S(2)}) collective-permute-start(bf16[256,1024]{0,1:T(8,128)(2,1)S(1)} %copy.106), channel_id=1, source_target_pairs={{28,0},{0,4},{4,8},{8,12},{12,16},{16,20},{20,24},{24,28},{29,1},{... | collective-permute-start | bytes 1572872 | tf_op jit(solution)/shard_map/while/body/eval_jaxpr/ppermute | solution.py:13
  398.7 49.3 %collective-permute-start.1 = (bf16[256,1024]{0,1:T(8,128)(2,1)}, bf16[256,1024]{0,1:T(8,128)(2,1)}, u32[]{:S(2)}, u32[]{:S(2)}) collective-permute-start(bf16[256,1024]{0,1:T(8,128)(2,1)} %copy.107), channel_id=1, source_target_pairs={{28,0},{0,4},{4,8},{8,12},{12,16},{16,20},{20,24},{24,28},{29,1},{... | collective-permute-start | bytes 1572872 | tf_op jit(solution)/shard_map/while/body/eval_jaxpr/ppermute | solution.py:13
  406.4 29.0 %collective-permute-start.2 = (bf16[256,1024]{0,1:T(8,128)(2,1)}, bf16[256,1024]{0,1:T(8,128)(2,1)}, u32[]{:S(2)}, u32[]{:S(2)}) collective-permute-start(bf16[256,1024]{0,1:T(8,128)(2,1)} %fusion.169), channel_id=1, source_target_pairs={{28,0},{0,4},{4,8},{8,12},{12,16},{16,20},{20,24},{24,28},{29,1},{... | collective-permute-start | bytes 1572872 | tf_op jit(solution)/shard_map/while/body/eval_jaxpr/ppermute | solution.py:13
  411.2 34.8 %collective-permute-start.3 = (bf16[256,1024]{0,1:T(8,128)(2,1)}, bf16[256,1024]{0,1:T(8,128)(2,1)}, u32[]{:S(2)}, u32[]{:S(2)}) collective-permute-start(bf16[256,1024]{0,1:T(8,128)(2,1)} %fusion.171), channel_id=1, source_target_pairs={{28,0},{0,4},{4,8},{8,12},{12,16},{16,20},{20,24},{24,28},{29,1},{... | collective-permute-start | bytes 1572872 | tf_op jit(solution)/shard_map/while/body/eval_jaxpr/ppermute | solution.py:13
  413.4 34.7 %copy-start.22 = (bf16[256,1024]{0,1:T(8,128)(2,1)S(1)}, bf16[256,1024]{0,1:T(8,128)(2,1)}, u32[]{:S(2)}) copy-start(bf16[256,1024]{0,1:T(8,128)(2,1)} %copy-done.21) | copy-start | bytes 1572868 | tf_op jit(solution)/shard_map/while
  449.3 51.9 %collective-permute-start = (bf16[256,1024]{0,1:T(8,128)(2,1)S(1)}, bf16[256,1024]{0,1:T(8,128)(2,1)}, u32[]{:S(2)}, u32[]{:S(2)}) collective-permute-start(bf16[256,1024]{0,1:T(8,128)(2,1)S(1)} %copy.106), channel_id=1, source_target_pairs={{28,0},{0,4},{4,8},{8,12},{12,16},{16,20},{20,24},{24,28},{29,1},{... | collective-permute-start | bytes 1572872 | tf_op jit(solution)/shard_map/while/body/eval_jaxpr/ppermute | solution.py:13
  451.2 50.0 %collective-permute-start.1 = (bf16[256,1024]{0,1:T(8,128)(2,1)}, bf16[256,1024]{0,1:T(8,128)(2,1)}, u32[]{:S(2)}, u32[]{:S(2)}) collective-permute-start(bf16[256,1024]{0,1:T(8,128)(2,1)} %copy.107), channel_id=1, source_target_pairs={{28,0},{0,4},{4,8},{8,12},{12,16},{16,20},{20,24},{24,28},{29,1},{... | collective-permute-start | bytes 1572872 | tf_op jit(solution)/shard_map/while/body/eval_jaxpr/ppermute | solution.py:13
  458.6 30.9 %collective-permute-start.2 = (bf16[256,1024]{0,1:T(8,128)(2,1)}, bf16[256,1024]{0,1:T(8,128)(2,1)}, u32[]{:S(2)}, u32[]{:S(2)}) collective-permute-start(bf16[256,1024]{0,1:T(8,128)(2,1)} %fusion.169), channel_id=1, source_target_pairs={{28,0},{0,4},{4,8},{8,12},{12,16},{16,20},{20,24},{24,28},{29,1},{... | collective-permute-start | bytes 1572872 | tf_op jit(solution)/shard_map/while/body/eval_jaxpr/ppermute | solution.py:13
  462.5 36.7 %collective-permute-start.3 = (bf16[256,1024]{0,1:T(8,128)(2,1)}, bf16[256,1024]{0,1:T(8,128)(2,1)}, u32[]{:S(2)}, u32[]{:S(2)}) collective-permute-start(bf16[256,1024]{0,1:T(8,128)(2,1)} %fusion.171), channel_id=1, source_target_pairs={{28,0},{0,4},{4,8},{8,12},{12,16},{16,20},{20,24},{24,28},{29,1},{... | collective-permute-start | bytes 1572872 | tf_op jit(solution)/shard_map/while/body/eval_jaxpr/ppermute | solution.py:13
  465.6 35.6 %copy-start.22 = (bf16[256,1024]{0,1:T(8,128)(2,1)S(1)}, bf16[256,1024]{0,1:T(8,128)(2,1)}, u32[]{:S(2)}) copy-start(bf16[256,1024]{0,1:T(8,128)(2,1)} %copy-done.21) | copy-start | bytes 1572868 | tf_op jit(solution)/shard_map/while
  466.2 35.0 %copy-start.3 = (f32[256,1024]{0,1:T(8,128)}, f32[256,1024]{0,1:T(8,128)S(1)}, u32[]{:S(2)}) copy-start(f32[256,1024]{0,1:T(8,128)S(1)} %bitcast_add_fusion.4) | copy-start | bytes 3145732 | tf_op jit(solution)/shard_map/while
  502.5 50.9 %collective-permute-start = (bf16[256,1024]{0,1:T(8,128)(2,1)S(1)}, bf16[256,1024]{0,1:T(8,128)(2,1)}, u32[]{:S(2)}, u32[]{:S(2)}) collective-permute-start(bf16[256,1024]{0,1:T(8,128)(2,1)S(1)} %copy.106), channel_id=1, source_target_pairs={{28,0},{0,4},{4,8},{8,12},{12,16},{16,20},{20,24},{24,28},{29,1},{... | collective-permute-start | bytes 1572872 | tf_op jit(solution)/shard_map/while/body/eval_jaxpr/ppermute | solution.py:13
  504.4 49.1 %collective-permute-start.1 = (bf16[256,1024]{0,1:T(8,128)(2,1)}, bf16[256,1024]{0,1:T(8,128)(2,1)}, u32[]{:S(2)}, u32[]{:S(2)}) collective-permute-start(bf16[256,1024]{0,1:T(8,128)(2,1)} %copy.107), channel_id=1, source_target_pairs={{28,0},{0,4},{4,8},{8,12},{12,16},{16,20},{20,24},{24,28},{29,1},{... | collective-permute-start | bytes 1572872 | tf_op jit(solution)/shard_map/while/body/eval_jaxpr/ppermute | solution.py:13
  510.6 32.0 %collective-permute-start.2 = (bf16[256,1024]{0,1:T(8,128)(2,1)}, bf16[256,1024]{0,1:T(8,128)(2,1)}, u32[]{:S(2)}, u32[]{:S(2)}) collective-permute-start(bf16[256,1024]{0,1:T(8,128)(2,1)} %fusion.169), channel_id=1, source_target_pairs={{28,0},{0,4},{4,8},{8,12},{12,16},{16,20},{20,24},{24,28},{29,1},{... | collective-permute-start | bytes 1572872 | tf_op jit(solution)/shard_map/while/body/eval_jaxpr/ppermute | solution.py:13
  513.9 37.4 %collective-permute-start.3 = (bf16[256,1024]{0,1:T(8,128)(2,1)}, bf16[256,1024]{0,1:T(8,128)(2,1)}, u32[]{:S(2)}, u32[]{:S(2)}) collective-permute-start(bf16[256,1024]{0,1:T(8,128)(2,1)} %fusion.171), channel_id=1, source_target_pairs={{28,0},{0,4},{4,8},{8,12},{12,16},{16,20},{20,24},{24,28},{29,1},{... | collective-permute-start | bytes 1572872 | tf_op jit(solution)/shard_map/while/body/eval_jaxpr/ppermute | solution.py:13
  516.9 36.5 %copy-start.22 = (bf16[256,1024]{0,1:T(8,128)(2,1)S(1)}, bf16[256,1024]{0,1:T(8,128)(2,1)}, u32[]{:S(2)}) copy-start(bf16[256,1024]{0,1:T(8,128)(2,1)} %copy-done.21) | copy-start | bytes 1572868 | tf_op jit(solution)/shard_map/while
  517.6 35.8 %copy-start.3 = (f32[256,1024]{0,1:T(8,128)}, f32[256,1024]{0,1:T(8,128)S(1)}, u32[]{:S(2)}) copy-start(f32[256,1024]{0,1:T(8,128)S(1)} %bitcast_add_fusion.4) | copy-start | bytes 3145732 | tf_op jit(solution)/shard_map/while
  554.7 50.0 %collective-permute-start = (bf16[256,1024]{0,1:T(8,128)(2,1)S(1)}, bf16[256,1024]{0,1:T(8,128)(2,1)}, u32[]{:S(2)}, u32[]{:S(2)}) collective-permute-start(bf16[256,1024]{0,1:T(8,128)(2,1)S(1)} %copy.106), channel_id=1, source_target_pairs={{28,0},{0,4},{4,8},{8,12},{12,16},{16,20},{20,24},{24,28},{29,1},{... | collective-permute-start | bytes 1572872 | tf_op jit(solution)/shard_map/while/body/eval_jaxpr/ppermute | solution.py:13
  556.6 48.1 %collective-permute-start.1 = (bf16[256,1024]{0,1:T(8,128)(2,1)}, bf16[256,1024]{0,1:T(8,128)(2,1)}, u32[]{:S(2)}, u32[]{:S(2)}) collective-permute-start(bf16[256,1024]{0,1:T(8,128)(2,1)} %copy.107), channel_id=1, source_target_pairs={{28,0},{0,4},{4,8},{8,12},{12,16},{16,20},{20,24},{24,28},{29,1},{... | collective-permute-start | bytes 1572872 | tf_op jit(solution)/shard_map/while/body/eval_jaxpr/ppermute | solution.py:13
  562.8 32.0 %collective-permute-start.2 = (bf16[256,1024]{0,1:T(8,128)(2,1)}, bf16[256,1024]{0,1:T(8,128)(2,1)}, u32[]{:S(2)}, u32[]{:S(2)}) collective-permute-start(bf16[256,1024]{0,1:T(8,128)(2,1)} %fusion.169), channel_id=1, source_target_pairs={{28,0},{0,4},{4,8},{8,12},{12,16},{16,20},{20,24},{24,28},{29,1},{... | collective-permute-start | bytes 1572872 | tf_op jit(solution)/shard_map/while/body/eval_jaxpr/ppermute | solution.py:13
  566.1 36.5 %collective-permute-start.3 = (bf16[256,1024]{0,1:T(8,128)(2,1)}, bf16[256,1024]{0,1:T(8,128)(2,1)}, u32[]{:S(2)}, u32[]{:S(2)}) collective-permute-start(bf16[256,1024]{0,1:T(8,128)(2,1)} %fusion.171), channel_id=1, source_target_pairs={{28,0},{0,4},{4,8},{8,12},{12,16},{16,20},{20,24},{24,28},{29,1},{... | collective-permute-start | bytes 1572872 | tf_op jit(solution)/shard_map/while/body/eval_jaxpr/ppermute | solution.py:13
  567.3 37.4 %copy-start.22 = (bf16[256,1024]{0,1:T(8,128)(2,1)S(1)}, bf16[256,1024]{0,1:T(8,128)(2,1)}, u32[]{:S(2)}) copy-start(bf16[256,1024]{0,1:T(8,128)(2,1)} %copy-done.21) | copy-start | bytes 1572868 | tf_op jit(solution)/shard_map/while
  568.0 36.7 %copy-start.3 = (f32[256,1024]{0,1:T(8,128)}, f32[256,1024]{0,1:T(8,128)S(1)}, u32[]{:S(2)}) copy-start(f32[256,1024]{0,1:T(8,128)S(1)} %bitcast_add_fusion.4) | copy-start | bytes 3145732 | tf_op jit(solution)/shard_map/while
  606.0 49.1 %collective-permute-start = (bf16[256,1024]{0,1:T(8,128)(2,1)S(1)}, bf16[256,1024]{0,1:T(8,128)(2,1)}, u32[]{:S(2)}, u32[]{:S(2)}) collective-permute-start(bf16[256,1024]{0,1:T(8,128)(2,1)S(1)} %copy.106), channel_id=1, source_target_pairs={{28,0},{0,4},{4,8},{8,12},{12,16},{16,20},{20,24},{24,28},{29,1},{... | collective-permute-start | bytes 1572872 | tf_op jit(solution)/shard_map/while/body/eval_jaxpr/ppermute | solution.py:13
  607.8 47.2 %collective-permute-start.1 = (bf16[256,1024]{0,1:T(8,128)(2,1)}, bf16[256,1024]{0,1:T(8,128)(2,1)}, u32[]{:S(2)}, u32[]{:S(2)}) collective-permute-start(bf16[256,1024]{0,1:T(8,128)(2,1)} %copy.107), channel_id=1, source_target_pairs={{28,0},{0,4},{4,8},{8,12},{12,16},{16,20},{20,24},{24,28},{29,1},{... | collective-permute-start | bytes 1572872 | tf_op jit(solution)/shard_map/while/body/eval_jaxpr/ppermute | solution.py:13
  614.1 32.0 %collective-permute-start.2 = (bf16[256,1024]{0,1:T(8,128)(2,1)}, bf16[256,1024]{0,1:T(8,128)(2,1)}, u32[]{:S(2)}, u32[]{:S(2)}) collective-permute-start(bf16[256,1024]{0,1:T(8,128)(2,1)} %fusion.169), channel_id=1, source_target_pairs={{28,0},{0,4},{4,8},{8,12},{12,16},{16,20},{20,24},{24,28},{29,1},{... | collective-permute-start | bytes 1572872 | tf_op jit(solution)/shard_map/while/body/eval_jaxpr/ppermute | solution.py:13
  617.4 35.5 %collective-permute-start.3 = (bf16[256,1024]{0,1:T(8,128)(2,1)}, bf16[256,1024]{0,1:T(8,128)(2,1)}, u32[]{:S(2)}, u32[]{:S(2)}) collective-permute-start(bf16[256,1024]{0,1:T(8,128)(2,1)} %fusion.171), channel_id=1, source_target_pairs={{28,0},{0,4},{4,8},{8,12},{12,16},{16,20},{20,24},{24,28},{29,1},{... | collective-permute-start | bytes 1572872 | tf_op jit(solution)/shard_map/while/body/eval_jaxpr/ppermute | solution.py:13
  618.2 36.9 %copy-start.22 = (bf16[256,1024]{0,1:T(8,128)(2,1)S(1)}, bf16[256,1024]{0,1:T(8,128)(2,1)}, u32[]{:S(2)}) copy-start(bf16[256,1024]{0,1:T(8,128)(2,1)} %copy-done.21) | copy-start | bytes 1572868 | tf_op jit(solution)/shard_map/while
  618.8 36.2 %copy-start.3 = (f32[256,1024]{0,1:T(8,128)}, f32[256,1024]{0,1:T(8,128)S(1)}, u32[]{:S(2)}) copy-start(f32[256,1024]{0,1:T(8,128)S(1)} %bitcast_add_fusion.4) | copy-start | bytes 3145732 | tf_op jit(solution)/shard_map/while
  656.3 48.1 %collective-permute-start = (bf16[256,1024]{0,1:T(8,128)(2,1)S(1)}, bf16[256,1024]{0,1:T(8,128)(2,1)}, u32[]{:S(2)}, u32[]{:S(2)}) collective-permute-start(bf16[256,1024]{0,1:T(8,128)(2,1)S(1)} %copy.106), channel_id=1, source_target_pairs={{28,0},{0,4},{4,8},{8,12},{12,16},{16,20},{20,24},{24,28},{29,1},{... | collective-permute-start | bytes 1572872 | tf_op jit(solution)/shard_map/while/body/eval_jaxpr/ppermute | solution.py:13
  658.2 46.3 %collective-permute-start.1 = (bf16[256,1024]{0,1:T(8,128)(2,1)}, bf16[256,1024]{0,1:T(8,128)(2,1)}, u32[]{:S(2)}, u32[]{:S(2)}) collective-permute-start(bf16[256,1024]{0,1:T(8,128)(2,1)} %copy.107), channel_id=1, source_target_pairs={{28,0},{0,4},{4,8},{8,12},{12,16},{16,20},{20,24},{24,28},{29,1},{... | collective-permute-start | bytes 1572872 | tf_op jit(solution)/shard_map/while/body/eval_jaxpr/ppermute | solution.py:13
  664.4 32.0 %collective-permute-start.2 = (bf16[256,1024]{0,1:T(8,128)(2,1)}, bf16[256,1024]{0,1:T(8,128)(2,1)}, u32[]{:S(2)}, u32[]{:S(2)}) collective-permute-start(bf16[256,1024]{0,1:T(8,128)(2,1)} %fusion.169), channel_id=1, source_target_pairs={{28,0},{0,4},{4,8},{8,12},{12,16},{16,20},{20,24},{24,28},{29,1},{... | collective-permute-start | bytes 1572872 | tf_op jit(solution)/shard_map/while/body/eval_jaxpr/ppermute | solution.py:13
  667.7 34.6 %collective-permute-start.3 = (bf16[256,1024]{0,1:T(8,128)(2,1)}, bf16[256,1024]{0,1:T(8,128)(2,1)}, u32[]{:S(2)}, u32[]{:S(2)}) collective-permute-start(bf16[256,1024]{0,1:T(8,128)(2,1)} %fusion.171), channel_id=1, source_target_pairs={{28,0},{0,4},{4,8},{8,12},{12,16},{16,20},{20,24},{24,28},{29,1},{... | collective-permute-start | bytes 1572872 | tf_op jit(solution)/shard_map/while/body/eval_jaxpr/ppermute | solution.py:13
  668.5 36.0 %copy-start.22 = (bf16[256,1024]{0,1:T(8,128)(2,1)S(1)}, bf16[256,1024]{0,1:T(8,128)(2,1)}, u32[]{:S(2)}) copy-start(bf16[256,1024]{0,1:T(8,128)(2,1)} %copy-done.21) | copy-start | bytes 1572868 | tf_op jit(solution)/shard_map/while
  669.2 35.3 %copy-start.3 = (f32[256,1024]{0,1:T(8,128)}, f32[256,1024]{0,1:T(8,128)S(1)}, u32[]{:S(2)}) copy-start(f32[256,1024]{0,1:T(8,128)S(1)} %bitcast_add_fusion.4) | copy-start | bytes 3145732 | tf_op jit(solution)/shard_map/while
  705.7 47.2 %collective-permute-start = (bf16[256,1024]{0,1:T(8,128)(2,1)S(1)}, bf16[256,1024]{0,1:T(8,128)(2,1)}, u32[]{:S(2)}, u32[]{:S(2)}) collective-permute-start(bf16[256,1024]{0,1:T(8,128)(2,1)S(1)} %copy.106), channel_id=1, source_target_pairs={{28,0},{0,4},{4,8},{8,12},{12,16},{16,20},{20,24},{24,28},{29,1},{... | collective-permute-start | bytes 1572872 | tf_op jit(solution)/shard_map/while/body/eval_jaxpr/ppermute | solution.py:13
  707.6 45.4 %collective-permute-start.1 = (bf16[256,1024]{0,1:T(8,128)(2,1)}, bf16[256,1024]{0,1:T(8,128)(2,1)}, u32[]{:S(2)}, u32[]{:S(2)}) collective-permute-start(bf16[256,1024]{0,1:T(8,128)(2,1)} %copy.107), channel_id=1, source_target_pairs={{28,0},{0,4},{4,8},{8,12},{12,16},{16,20},{20,24},{24,28},{29,1},{... | collective-permute-start | bytes 1572872 | tf_op jit(solution)/shard_map/while/body/eval_jaxpr/ppermute | solution.py:13
  713.8 31.4 %collective-permute-start.2 = (bf16[256,1024]{0,1:T(8,128)(2,1)}, bf16[256,1024]{0,1:T(8,128)(2,1)}, u32[]{:S(2)}, u32[]{:S(2)}) collective-permute-start(bf16[256,1024]{0,1:T(8,128)(2,1)} %fusion.169), channel_id=1, source_target_pairs={{28,0},{0,4},{4,8},{8,12},{12,16},{16,20},{20,24},{24,28},{29,1},{... | collective-permute-start | bytes 1572872 | tf_op jit(solution)/shard_map/while/body/eval_jaxpr/ppermute | solution.py:13
  717.2 33.7 %collective-permute-start.3 = (bf16[256,1024]{0,1:T(8,128)(2,1)}, bf16[256,1024]{0,1:T(8,128)(2,1)}, u32[]{:S(2)}, u32[]{:S(2)}) collective-permute-start(bf16[256,1024]{0,1:T(8,128)(2,1)} %fusion.171), channel_id=1, source_target_pairs={{28,0},{0,4},{4,8},{8,12},{12,16},{16,20},{20,24},{24,28},{29,1},{... | collective-permute-start | bytes 1572872 | tf_op jit(solution)/shard_map/while/body/eval_jaxpr/ppermute | solution.py:13
  717.9 35.0 %copy-start.22 = (bf16[256,1024]{0,1:T(8,128)(2,1)S(1)}, bf16[256,1024]{0,1:T(8,128)(2,1)}, u32[]{:S(2)}) copy-start(bf16[256,1024]{0,1:T(8,128)(2,1)} %copy-done.21) | copy-start | bytes 1572868 | tf_op jit(solution)/shard_map/while
  718.6 34.3 %copy-start.3 = (f32[256,1024]{0,1:T(8,128)}, f32[256,1024]{0,1:T(8,128)S(1)}, u32[]{:S(2)}) copy-start(f32[256,1024]{0,1:T(8,128)S(1)} %bitcast_add_fusion.4) | copy-start | bytes 3145732 | tf_op jit(solution)/shard_map/while
  754.2 46.3 %collective-permute-start = (bf16[256,1024]{0,1:T(8,128)(2,1)S(1)}, bf16[256,1024]{0,1:T(8,128)(2,1)}, u32[]{:S(2)}, u32[]{:S(2)}) collective-permute-start(bf16[256,1024]{0,1:T(8,128)(2,1)S(1)} %copy.106), channel_id=1, source_target_pairs={{28,0},{0,4},{4,8},{8,12},{12,16},{16,20},{20,24},{24,28},{29,1},{... | collective-permute-start | bytes 1572872 | tf_op jit(solution)/shard_map/while/body/eval_jaxpr/ppermute | solution.py:13
  756.1 44.4 %collective-permute-start.1 = (bf16[256,1024]{0,1:T(8,128)(2,1)}, bf16[256,1024]{0,1:T(8,128)(2,1)}, u32[]{:S(2)}, u32[]{:S(2)}) collective-permute-start(bf16[256,1024]{0,1:T(8,128)(2,1)} %copy.107), channel_id=1, source_target_pairs={{28,0},{0,4},{4,8},{8,12},{12,16},{16,20},{20,24},{24,28},{29,1},{... | collective-permute-start | bytes 1572872 | tf_op jit(solution)/shard_map/while/body/eval_jaxpr/ppermute | solution.py:13
  762.3 30.5 %collective-permute-start.2 = (bf16[256,1024]{0,1:T(8,128)(2,1)}, bf16[256,1024]{0,1:T(8,128)(2,1)}, u32[]{:S(2)}, u32[]{:S(2)}) collective-permute-start(bf16[256,1024]{0,1:T(8,128)(2,1)} %fusion.169), channel_id=1, source_target_pairs={{28,0},{0,4},{4,8},{8,12},{12,16},{16,20},{20,24},{24,28},{29,1},{... | collective-permute-start | bytes 1572872 | tf_op jit(solution)/shard_map/while/body/eval_jaxpr/ppermute | solution.py:13
  765.7 32.8 %collective-permute-start.3 = (bf16[256,1024]{0,1:T(8,128)(2,1)}, bf16[256,1024]{0,1:T(8,128)(2,1)}, u32[]{:S(2)}, u32[]{:S(2)}) collective-permute-start(bf16[256,1024]{0,1:T(8,128)(2,1)} %fusion.171), channel_id=1, source_target_pairs={{28,0},{0,4},{4,8},{8,12},{12,16},{16,20},{20,24},{24,28},{29,1},{... | collective-permute-start | bytes 1572872 | tf_op jit(solution)/shard_map/while/body/eval_jaxpr/ppermute | solution.py:13
  804.1 70.5 %reduce-scatter.9.cloned.1.call-start = ((), (), s32[]{:S(2)}) async-start(), calls=%async_computation.15 | async-start | bytes 2621440 | tf_op jit(solution)/shard_map/reduce_scatter | solution.py:108
  806.3 95.1 %reduce-scatter.11.cloned.1.call-start = ((), (), s32[]{:S(2)}) async-start(), calls=%async_computation.16 | async-start | bytes 2621440 | tf_op jit(solution)/shard_map/reduce_scatter | solution.py:108
  808.4 127.0 %reduce-scatter.13.cloned.1.call-start = ((), (), s32[]{:S(2)}) async-start(), calls=%async_computation.17 | async-start | bytes 2621440 | tf_op jit(solution)/shard_map/reduce_scatter | solution.py:108
  812.1 197.6 %reduce-scatter.15.cloned.1.call-start = ((), (), s32[]{:S(2)}) async-start(), calls=%async_computation.18 | async-start | bytes 10485760 | tf_op jit(solution)/shard_map/reduce_scatter | solution.py:108
  819.6 264.5 %reduce-scatter.17.cloned.1.call-start = ((), (), s32[]{:S(2)}) async-start(), calls=%async_computation.19 | async-start | bytes 10485760 | tf_op jit(solution)/shard_map/reduce_scatter | solution.py:108
  (66 other events, 447.6 us)
Sparse Core Ops, SparseCore 0:
  9.6 25.2 all-gather.8
  36.5 22.5 all-gather.14
  60.7 22.5 all-gather.12
  85.8 73.4 all-gather.10
  161.9 71.6 all-gather.16
  235.0 20.8 all-gather.18
  257.4 58.2 all-gather.20
  317.3 58.2 all-gather.22
  804.2 27.9 reduce-scatter.6
  834.8 32.4 reduce-scatter.8
  869.8 31.5 reduce-scatter.10
  903.9 31.3 reduce-scatter.12
  938.0 71.7 reduce-scatter.14
  1012.3 71.7 reduce-scatter.16
where the time goes:
time: 1590 us; the launch traced here: 1580 us
  waiting for transfers between devices  689 us (43%)
  blocking collectives  524 us (33%)
  matrix products  194 us (12%)
  other arithmetic  85.1 us (5%)
  local copies, waits for them, and re-layouts  59 us (4%)
    psum x1, blocking collectives, body(): lax.psum((share_query, share_key, share_value, share_out, share_up, share...  485 us
    ppermute x32, waiting for transfers between devices, from_behind(): return lax.ppermute(block, axis, route)  247 us
    reduce_scatter x6, waiting for transfers between devices, owner_rows(): lax.psum_scatter(lax.dot_general(layer_in, layer_grad, (((0,), (0,)), (()...  209 us
    all_gather x1, waiting for transfers between devices, body(): value_piece = lax.all_gather(values, 'ctx', axis=0, tiled=True)  74.2 us
    all_gather x1, waiting for transfers between devices, body(): key_piece = lax.all_gather(key_rows, 'ctx', axis=0, tiled=True)  73.5 us
    psum x1, blocking collectives, body(): lax.psum((grad_query_b, grad_value_b, grad_output_b, grad_attn_gain, grad...  38.5 us
    dot_general x8, matrix products, online_update(): jnp.einsum('hqk,khd->qhd', exp_scores.astype(jnp.bfloat16), value_rows.re...  37.9 us
    while x120, local copies, waits for them, and re-layouts  34.6 us
  transfers between devices with their start and end apart: 46, of which 26 were waited for; matrix products, arithmetic and copies ran while one was open for 18% of the time, Pallas kernels for 0%

commit v1 on v0

--- a/solution.py
+++ b/solution.py
@@ -178,8 +178,11 @@
         jnp.full((H, block_len), -1e30, jnp.float32),
         jnp.zeros((H, block_len), jnp.float32),
     )
-    key_piece = lax.all_gather(key_rows, "ctx", axis=0, tiled=True)
-    value_piece = lax.all_gather(values, "ctx", axis=0, tiled=True)
+    key_piece, value_piece = jnp.split(
+        lax.all_gather(jnp.concatenate([key_rows, values], axis=1), "ctx", axis=0, tiled=True),
+        [key_rows.shape[1]],
+        axis=1,
+    )
     shards = key_piece.shape[0] // block_len
 
     def one_shard(index, inner):

time: 1590 us -> 1530 us (0.962)
  waiting for transfers between devices: 689 us -> 630 us
    reduce_scatter x6, waiting for transfers between devices: 209 us -> 178 us  [owner_rows(): lax.psum_scatter(lax.dot_general(layer_in, layer_grad, (((0,), (0,)), (()...]
    all_gather x2 -> x1, waiting for transfers between devices: 148 us -> 125 us  [body(): lax.all_gather(jnp.concatenate([key_rows, values], axis=1), 'ctx', axis=0...]
  transfers between devices with their start and end apart: 46 -> 45, of which waited for: 26 -> 24; matrix products, arithmetic and copies ran while one was open for 18% -> 20% of each run, Pallas kernels for 0% -> 0%
where the time goes in v1:
time: 1530 us
  waiting for transfers between devices  630 us (41%)
  blocking collectives  524 us (34%)
  matrix products  194 us (13%)
  other arithmetic  84.6 us (6%)
  local copies, waits for them, and re-layouts  66 us (4%)
    psum x1, blocking collectives, body(): lax.psum((share_query, share_key, share_value, share_out, share_up, share...  485 us
    ppermute x32, waiting for transfers between devices, from_behind(): return lax.ppermute(block, axis, route)  247 us
    reduce_scatter x6, waiting for transfers between devices, owner_rows(): lax.psum_scatter(lax.dot_general(layer_in, layer_grad, (((0,), (0,)), (()...  178 us
    all_gather x1, waiting for transfers between devices, body(): lax.all_gather(jnp.concatenate([key_rows, values], axis=1), 'ctx', axis=0...  125 us
    psum x1, blocking collectives, body(): lax.psum((grad_query_b, grad_value_b, grad_output_b, grad_attn_gain, grad...  38.7 us
    dot_general x8, matrix products, online_update(): jnp.einsum('hqk,khd->qhd', exp_scores.astype(jnp.bfloat16), value_rows.re...  37.5 us
    while x120, local copies, waits for them, and re-layouts  34.6 us
    dot_general x6, matrix products, dense(): return jnp.dot(left, right, preferred_element_type=jnp.float32)  32.1 us
  transfers between devices with their start and end apart: 45, of which 24 were waited for; matrix products, arithmetic and copies ran while one was open for 20% of the time, Pallas kernels for 0%

profile of v1, /device:TPU:0, one launch (start us, length us, event | category | flops | bytes accessed | tf_op | source)
XLA Modules:
  0.0 1527.5 jit_solution(4932184221859875297)
XLA Ops:
  9.5 25.4 %all-gather.8.cloned.1.call-done = bf16[1024,1024]{1,0:T(8,128)(2,1)} async-done(((bf16[256,1024]{1,0:T(8,128)(2,1)}), bf16[1024,1024]{1,0:T(8,128)(2,1)}) %all-gather.8.cloned.1.call-update) | async-done | bytes 2097168 | tf_op jit(solution)/shard_map/all_gather | solution.py:166
  37.4 21.7 %all-gather.10.cloned.1.call-done = bf16[1024,1024]{1,0:T(8,128)(2,1)} async-done(((bf16[256,1024]{1,0:T(8,128)(2,1)}), bf16[1024,1024]{1,0:T(8,128)(2,1)}) %all-gather.10.cloned.1.call-update) | async-done | bytes 2097168 | tf_op jit(solution)/shard_map/all_gather | solution.py:167
  68.1 15.2 all-gather.14.cloned.1.call-done
  85.8 125.0 %all-gather.12.cloned.1.call-done = bf16[2048,2048]{1,0:T(8,128)(2,1)} async-done(((bf16[256,2048]{1,0:T(8,128)(2,1)}), bf16[2048,2048]{1,0:T(8,128)(2,1)}) %all-gather.12.cloned.1.call-update) | async-done | bytes 8388624 | tf_op jit(solution)/shard_map/all_gather | solution.py:182
  210.8 6.3 fusion.87
  217.1 101.5 %while.42 = (s32[]{:T(128)}, f32[256,16,64]{0,2,1:T(8,128)}, f32[16,256]{1,0:T(8,128)S(1)}, f32[16,256]{1,0:T(8,128)S(1)}, s32[256]{0:T(256)S(1)}, /*index=5*/s3...) while((s32[]{:T(128)}, f32[256,16,64]{0,2,1:T(8,128)}, ...), condition=%wide.region_6.7_spmd.clone, body=%wide.region_3.6_spmd.clone.sunk | while | flops 282943488 | bytes 20975804 | solution.py:194
  221.6 3.2 fusion.157
  225.1 4.3 fusion.156
  233.9 3.2 fusion.157
  237.3 4.6 fusion.156
  243.7 3.3 fusion.154
  247.0 3.2 fusion.157
  250.5 4.6 fusion.156
  256.8 2.8 fusion.154
  259.6 3.2 fusion.157
  263.0 4.7 fusion.156
  272.2 3.2 fusion.157
  275.6 4.6 fusion.156
  284.7 3.2 fusion.157
  288.2 4.6 fusion.156
  294.5 2.8 fusion.154
  297.3 3.2 fusion.157
  300.7 5.4 fusion.156
  310.6 3.2 fusion.157
  314.0 4.6 fusion.156
  322.8 15.9 %fusion.29 = (bf16[256,4096]{1,0:T(8,128)(2,1)}, f32[256,4096]{1,0:T(8,128)}) fusion(f32[4096]{0:T(1024)S(1)} %copy-done.28, bf16[1024,4096]{1,0:T(8,128)(2,1)} %all-gather.18.cloned.1.call-done, f32[256,1024]{1,0:T(8,128)S(1)} %get-tuple-element.760, f32[1024]{0:T(1024)S(1)} %copy-done.23, f32[1024]{0:T(1024)S(1)} %copy-done.22, ...), kind=kOutput, calls=%fused_computation.46 | convolution fusion | flops 2218000384 | bytes 15755264 | tf_op jit(solution)/shard_map/dot_general | solution.py:17
  338.8 13.9 all-gather.20.cloned.1.call-done
  352.7 6.6 fusion.89
  361.5 4.2 convert_reduce_fusion
  370.9 3.1 convolution_convert_fusion.3
  375.6 406.6 %while.43 = (s32[]{:T(128)}, bf16[256,1024]{0,1:T(8,128)(2,1)}, bf16[256,1024]{0,1:T(8,128)(2,1)}, f32[256,1024]{0,1:T(8,128)}, f32[256,1024]{0,1:T(8,128)}, /*i...) while((s32[]{:T(128)}, bf16[256,1024]{0,1:T(8,128)(2,1)}, ...), condition=%wide.region_16.17_spmd.clone, body=%wide.region_15.16_spmd.clone.sunk | while | flops 686882816 | bytes 68932264 | solution.py:241
  382.8 3.2 multiply_convert_fusion.2
  395.8 21.2 %collective-permute-done.2 = bf16[256,1024]{0,1:T(8,128)(2,1)} collective-permute-done((bf16[256,1024]{0,1:T(8,128)(2,1)}, bf16[256,1024]{0,1:T(8,128)(2,1)}, u32[]{:S(2)}, u32[]{:S(2)}) %collective-permute-start.2) | collective-permute-done | bytes 524320 | tf_op jit(solution)/shard_map/while/body/eval_jaxpr/ppermute | solution.py:13
  419.1 8.5 collective-permute-done.3
  434.9 3.1 multiply_convert_fusion.2
  447.8 23.2 %collective-permute-done.2 = bf16[256,1024]{0,1:T(8,128)(2,1)} collective-permute-done((bf16[256,1024]{0,1:T(8,128)(2,1)}, bf16[256,1024]{0,1:T(8,128)(2,1)}, u32[]{:S(2)}, u32[]{:S(2)}) %collective-permute-start.2) | collective-permute-done | bytes 524320 | tf_op jit(solution)/shard_map/while/body/eval_jaxpr/ppermute | solution.py:13
  473.2 7.6 collective-permute-done.3
  486.9 3.1 multiply_convert_fusion.2
  499.2 25.0 %collective-permute-done.2 = bf16[256,1024]{0,1:T(8,128)(2,1)} collective-permute-done((bf16[256,1024]{0,1:T(8,128)(2,1)}, bf16[256,1024]{0,1:T(8,128)(2,1)}, u32[]{:S(2)}, u32[]{:S(2)}) %collective-permute-start.2) | collective-permute-done | bytes 524320 | tf_op jit(solution)/shard_map/while/body/eval_jaxpr/ppermute | solution.py:13
  526.3 6.6 collective-permute-done.3
  539.1 3.1 multiply_convert_fusion.2
  549.6 26.8 %collective-permute-done.2 = bf16[256,1024]{0,1:T(8,128)(2,1)} collective-permute-done((bf16[256,1024]{0,1:T(8,128)(2,1)}, bf16[256,1024]{0,1:T(8,128)(2,1)}, u32[]{:S(2)}, u32[]{:S(2)}) %collective-permute-start.2) | collective-permute-done | bytes 524320 | tf_op jit(solution)/shard_map/while/body/eval_jaxpr/ppermute | solution.py:13
  578.5 5.7 collective-permute-done.3
  590.4 3.1 multiply_convert_fusion.2
  600.5 27.2 %collective-permute-done.2 = bf16[256,1024]{0,1:T(8,128)(2,1)} collective-permute-done((bf16[256,1024]{0,1:T(8,128)(2,1)}, bf16[256,1024]{0,1:T(8,128)(2,1)}, u32[]{:S(2)}, u32[]{:S(2)}) %collective-permute-start.2) | collective-permute-done | bytes 524320 | tf_op jit(solution)/shard_map/while/body/eval_jaxpr/ppermute | solution.py:13
  629.8 4.8 collective-permute-done.3
  640.8 3.1 multiply_convert_fusion.2
  650.8 27.2 %collective-permute-done.2 = bf16[256,1024]{0,1:T(8,128)(2,1)} collective-permute-done((bf16[256,1024]{0,1:T(8,128)(2,1)}, bf16[256,1024]{0,1:T(8,128)(2,1)}, u32[]{:S(2)}, u32[]{:S(2)}) %collective-permute-start.2) | collective-permute-done | bytes 524320 | tf_op jit(solution)/shard_map/while/body/eval_jaxpr/ppermute | solution.py:13
  680.1 3.8 collective-permute-done.3
  690.2 3.1 multiply_convert_fusion.2
  700.3 26.6 %collective-permute-done.2 = bf16[256,1024]{0,1:T(8,128)(2,1)} collective-permute-done((bf16[256,1024]{0,1:T(8,128)(2,1)}, bf16[256,1024]{0,1:T(8,128)(2,1)}, u32[]{:S(2)}, u32[]{:S(2)}) %collective-permute-start.2) | collective-permute-done | bytes 524320 | tf_op jit(solution)/shard_map/while/body/eval_jaxpr/ppermute | solution.py:13
  729.0 3.5 collective-permute-done.3
  738.7 3.1 multiply_convert_fusion.2
  748.8 25.7 %collective-permute-done.2 = bf16[256,1024]{0,1:T(8,128)(2,1)} collective-permute-done((bf16[256,1024]{0,1:T(8,128)(2,1)}, bf16[256,1024]{0,1:T(8,128)(2,1)}, u32[]{:S(2)}, u32[]{:S(2)}) %collective-permute-start.2) | collective-permute-done | bytes 524320 | tf_op jit(solution)/shard_map/while/body/eval_jaxpr/ppermute | solution.py:13
  776.5 3.5 collective-permute-done.3
  782.2 3.5 convert_bitcast_fusion.2
  787.9 3.1 convert_bitcast_fusion
  791.2 7.4 convolution_convert_fusion.1
  800.0 7.2 convolution_convert_fusion
  808.6 38.7 %all-reduce = (f32[1024]{0:T(1024)}, f32[1024]{0:T(1024)}, f32[1024]{0:T(1024)}, f32[1024]{0:T(1024)}, f32[1024]{0:T(1024)}, /*index=5*/f32[4096]{0:T(1024)}, f32[1024]{0:T(1024)}, f32[1024]{0:T(1024)}, f32[1024]{0:T(1024)}) all-reduce(f32[1024]{0:T(1024)S(1)} %convert_reduce_fusion.5, ...), channel_id=1, replica_groups=mesh['ctx'=8,'fsdp'=4] {'ctx','fsdp'}, use_global_device_ids=true, to_apply=%region_20.21 | all-reduce | flops 12288 | bytes 98304 | tf_op jit(solution)/shard_map/psum | solution.py:270
  854.0 29.0 %reduce-scatter.11.cloned.1.call-done = bf16[256,1024]{0,1:T(8,128)(2,1)} async-done(((bf16[1024,1024]{0,1:T(8,128)(2,1)}), bf16[256,1024]{0,1:T(8,128)(2,1)}) %reduce-scatter.11.cloned.1.call-update) | async-done | bytes 524304 | tf_op jit(solution)/shard_map/reduce_scatter | solution.py:108
  883.0 74.2 %reduce-scatter.15.cloned.1.call-done = bf16[256,4096]{1,0:T(8,128)(2,1)} async-done(((bf16[1024,4096]{1,0:T(8,128)(2,1)}), bf16[256,4096]{1,0:T(8,128)(2,1)}) %reduce-scatter.15.cloned.1.call-update) | async-done | bytes 2097168 | tf_op jit(solution)/shard_map/reduce_scatter | solution.py:108
  957.2 74.5 %reduce-scatter.17.cloned.1.call-done = bf16[1024,1024]{1,0:T(8,128)(2,1)} async-done(((bf16[4096,1024]{1,0:T(8,128)(2,1)}), bf16[1024,1024]{1,0:T(8,128)(2,1)}) %reduce-scatter.17.cloned.1.call-update) | async-done | bytes 2097168 | tf_op jit(solution)/shard_map/reduce_scatter | solution.py:108
  1031.7 485.2 %all-reduce.3 = (f32[256,1024]{0,1:T(8,128)S(1)}, f32[256,1024]{0,1:T(8,128)S(1)}, f32[256,1024]{0,1:T(8,128)S(1)}, f32[256,1024]{1,0:T(8,128)}, f32[256,4096]{1,0:T(8,128)}, /*index=5*/f32[1024,1024]{1,0:T(8,128)}) all-reduce(bf16[256,1024]{0,1:T(8,128)(2,1)} %reduce-scatter.7.cloned.1.call-done, ...), channel_id=1, replica_groups=mesh['ctx'=8,'fsdp'=4] {'ctx'}, use_global_device_ids=true, to_apply=%region_18.19 | all-reduce | flops 3145728 | bytes 18874368 | tf_op jit(solution)/shard_map/psum | solution.py:257
  (464 shorter events, 207.5 us)
Async XLA Ops:
  7.2 51.9 %copy-start.11 = (bf16[1,16,16,1024]{3,2,1,0:T(8,128)(2,1)S(1)}, bf16[1,16,16,1024]{3,2,1,0:T(8,128)(2,1)}, u32[]{:S(2)}) copy-start(bf16[1,16,16,1024]{3,2,1,0:T(8,128)(2,1)} %param.23) | copy-start | bytes 1572868
  7.2 51.9 %copy-start.29 = (f32[1024]{0:T(1024)S(1)}, f32[1024]{0:T(1024)}, u32[]{:S(2)}) copy-start(f32[1024]{0:T(1024)} %param.30) | copy-start | bytes 12292
  7.2 27.7 %all-gather.8.cloned.1.call-start = ((), (), s32[]{:S(2)}) async-start(), calls=%async_computation.6 | async-start | bytes 2621440 | tf_op jit(solution)/shard_map/all_gather | solution.py:166
  7.9 51.2 %all-gather.10.cloned.1.call-start = ((), (), s32[]{:S(2)}) async-start(), calls=%async_computation.7 | async-start | bytes 2621440 | tf_op jit(solution)/shard_map/all_gather | solution.py:167
  8.7 74.6 %all-gather.14.cloned.1.call-start = ((), (), s32[]{:S(2)}) async-start(), calls=%async_computation.9 | async-start | bytes 2621440 | tf_op jit(solution)/shard_map/all_gather | solution.py:165
  9.4 201.4 %all-gather.12.cloned.1.call-start = ((), (), s32[]{:S(2)}) async-start(), calls=%async_computation.8 | async-start | bytes 9437184 | tf_op jit(solution)/shard_map/all_gather | solution.py:182
  62.5 257.5 %all-gather.16.cloned.1.call-start = ((), (), s32[]{:S(2)}) async-start(), calls=%async_computation.10 | async-start | bytes 2621440 | tf_op jit(solution)/shard_map/all_gather | solution.py:168
  63.1 259.6 %all-gather.18.cloned.1.call-start = ((), (), s32[]{:S(2)}) async-start(), calls=%async_computation.11 | async-start | bytes 10485760 | tf_op jit(solution)/shard_map/all_gather | solution.py:169
  63.7 288.9 %all-gather.20.cloned.1.call-start = ((), (), s32[]{:S(2)}) async-start(), calls=%async_computation.12 | async-start | bytes 10485760 | tf_op jit(solution)/shard_map/all_gather | solution.py:170
  64.5 789.6 %reduce-scatter.13.cloned.1.call-start = ((), (), s32[]{:S(2)}) async-start(), calls=%async_computation.16 | async-start | bytes 2621440 | tf_op jit(solution)/shard_map/reduce_scatter | solution.py:108
  217.1 102.9 %copy-start.25 = (f32[1024]{0:T(1024)S(1)}, f32[1024]{0:T(1024)}, u32[]{:S(2)}) copy-start(f32[1024]{0:T(1024)} %param.32) | copy-start | bytes 12292
  322.5 46.0 %copy-start.7 = (f32[256,1024]{1,0:T(8,128)}, f32[256,1024]{1,0:T(8,128)S(1)}, u32[]{:S(2)}) copy-start(f32[256,1024]{1,0:T(8,128)S(1)} %get-tuple-element.760) | copy-start | bytes 3145732
  375.5 478.5 %reduce-scatter.7.cloned.1.call-start = ((), (), s32[]{:S(2)}) async-start(), calls=%async_computation.13 | async-start | bytes 2621440 | tf_op jit(solution)/shard_map/reduce_scatter | solution.py:108
  377.0 52.7 %collective-permute-start = (bf16[256,1024]{0,1:T(8,128)(2,1)S(1)}, bf16[256,1024]{0,1:T(8,128)(2,1)}, u32[]{:S(2)}, u32[]{:S(2)}) collective-permute-start(bf16[256,1024]{0,1:T(8,128)(2,1)S(1)} %copy.106), channel_id=1, source_target_pairs={{28,0},{0,4},{4,8},{8,12},{12,16},{16,20},{20,24},{24,28},{29,1},{... | collective-permute-start | bytes 1572872 | tf_op jit(solution)/shard_map/while/body/eval_jaxpr/ppermute | solution.py:13
  380.3 49.4 %collective-permute-start.1 = (bf16[256,1024]{0,1:T(8,128)(2,1)}, bf16[256,1024]{0,1:T(8,128)(2,1)}, u32[]{:S(2)}, u32[]{:S(2)}) collective-permute-start(bf16[256,1024]{0,1:T(8,128)(2,1)} %copy.107), channel_id=1, source_target_pairs={{28,0},{0,4},{4,8},{8,12},{12,16},{16,20},{20,24},{24,28},{29,1},{... | collective-permute-start | bytes 1572872 | tf_op jit(solution)/shard_map/while/body/eval_jaxpr/ppermute | solution.py:13
  388.1 28.9 %collective-permute-start.2 = (bf16[256,1024]{0,1:T(8,128)(2,1)}, bf16[256,1024]{0,1:T(8,128)(2,1)}, u32[]{:S(2)}, u32[]{:S(2)}) collective-permute-start(bf16[256,1024]{0,1:T(8,128)(2,1)} %fusion.170), channel_id=1, source_target_pairs={{28,0},{0,4},{4,8},{8,12},{12,16},{16,20},{20,24},{24,28},{29,1},{... | collective-permute-start | bytes 1572872 | tf_op jit(solution)/shard_map/while/body/eval_jaxpr/ppermute | solution.py:13
  392.9 34.7 %collective-permute-start.3 = (bf16[256,1024]{0,1:T(8,128)(2,1)}, bf16[256,1024]{0,1:T(8,128)(2,1)}, u32[]{:S(2)}, u32[]{:S(2)}) collective-permute-start(bf16[256,1024]{0,1:T(8,128)(2,1)} %fusion.172), channel_id=1, source_target_pairs={{28,0},{0,4},{4,8},{8,12},{12,16},{16,20},{20,24},{24,28},{29,1},{... | collective-permute-start | bytes 1572872 | tf_op jit(solution)/shard_map/while/body/eval_jaxpr/ppermute | solution.py:13
  395.1 34.6 %copy-start.21 = (bf16[256,1024]{0,1:T(8,128)(2,1)S(1)}, bf16[256,1024]{0,1:T(8,128)(2,1)}, u32[]{:S(2)}) copy-start(bf16[256,1024]{0,1:T(8,128)(2,1)} %copy-done.20) | copy-start | bytes 1572868 | tf_op jit(solution)/shard_map/while
  395.8 33.9 %copy-start.3 = (f32[256,1024]{0,1:T(8,128)}, f32[256,1024]{0,1:T(8,128)S(1)}, u32[]{:S(2)}) copy-start(f32[256,1024]{0,1:T(8,128)S(1)} %bitcast_add_fusion.4) | copy-start | bytes 3145732 | tf_op jit(solution)/shard_map/while
  430.9 51.9 %collective-permute-start = (bf16[256,1024]{0,1:T(8,128)(2,1)S(1)}, bf16[256,1024]{0,1:T(8,128)(2,1)}, u32[]{:S(2)}, u32[]{:S(2)}) collective-permute-start(bf16[256,1024]{0,1:T(8,128)(2,1)S(1)} %copy.106), channel_id=1, source_target_pairs={{28,0},{0,4},{4,8},{8,12},{12,16},{16,20},{20,24},{24,28},{29,1},{... | collective-permute-start | bytes 1572872 | tf_op jit(solution)/shard_map/while/body/eval_jaxpr/ppermute | solution.py:13
  432.8 50.0 %collective-permute-start.1 = (bf16[256,1024]{0,1:T(8,128)(2,1)}, bf16[256,1024]{0,1:T(8,128)(2,1)}, u32[]{:S(2)}, u32[]{:S(2)}) collective-permute-start(bf16[256,1024]{0,1:T(8,128)(2,1)} %copy.107), channel_id=1, source_target_pairs={{28,0},{0,4},{4,8},{8,12},{12,16},{16,20},{20,24},{24,28},{29,1},{... | collective-permute-start | bytes 1572872 | tf_op jit(solution)/shard_map/while/body/eval_jaxpr/ppermute | solution.py:13
  440.2 30.9 %collective-permute-start.2 = (bf16[256,1024]{0,1:T(8,128)(2,1)}, bf16[256,1024]{0,1:T(8,128)(2,1)}, u32[]{:S(2)}, u32[]{:S(2)}) collective-permute-start(bf16[256,1024]{0,1:T(8,128)(2,1)} %fusion.170), channel_id=1, source_target_pairs={{28,0},{0,4},{4,8},{8,12},{12,16},{16,20},{20,24},{24,28},{29,1},{... | collective-permute-start | bytes 1572872 | tf_op jit(solution)/shard_map/while/body/eval_jaxpr/ppermute | solution.py:13
  444.0 36.7 %collective-permute-start.3 = (bf16[256,1024]{0,1:T(8,128)(2,1)}, bf16[256,1024]{0,1:T(8,128)(2,1)}, u32[]{:S(2)}, u32[]{:S(2)}) collective-permute-start(bf16[256,1024]{0,1:T(8,128)(2,1)} %fusion.172), channel_id=1, source_target_pairs={{28,0},{0,4},{4,8},{8,12},{12,16},{16,20},{20,24},{24,28},{29,1},{... | collective-permute-start | bytes 1572872 | tf_op jit(solution)/shard_map/while/body/eval_jaxpr/ppermute | solution.py:13
  447.1 35.7 %copy-start.21 = (bf16[256,1024]{0,1:T(8,128)(2,1)S(1)}, bf16[256,1024]{0,1:T(8,128)(2,1)}, u32[]{:S(2)}) copy-start(bf16[256,1024]{0,1:T(8,128)(2,1)} %copy-done.20) | copy-start | bytes 1572868 | tf_op jit(solution)/shard_map/while
  447.8 35.0 %copy-start.3 = (f32[256,1024]{0,1:T(8,128)}, f32[256,1024]{0,1:T(8,128)S(1)}, u32[]{:S(2)}) copy-start(f32[256,1024]{0,1:T(8,128)S(1)} %bitcast_add_fusion.4) | copy-start | bytes 3145732 | tf_op jit(solution)/shard_map/while
  484.1 50.9 %collective-permute-start = (bf16[256,1024]{0,1:T(8,128)(2,1)S(1)}, bf16[256,1024]{0,1:T(8,128)(2,1)}, u32[]{:S(2)}, u32[]{:S(2)}) collective-permute-start(bf16[256,1024]{0,1:T(8,128)(2,1)S(1)} %copy.106), channel_id=1, source_target_pairs={{28,0},{0,4},{4,8},{8,12},{12,16},{16,20},{20,24},{24,28},{29,1},{... | collective-permute-start | bytes 1572872 | tf_op jit(solution)/shard_map/while/body/eval_jaxpr/ppermute | solution.py:13
  486.0 49.1 %collective-permute-start.1 = (bf16[256,1024]{0,1:T(8,128)(2,1)}, bf16[256,1024]{0,1:T(8,128)(2,1)}, u32[]{:S(2)}, u32[]{:S(2)}) collective-permute-start(bf16[256,1024]{0,1:T(8,128)(2,1)} %copy.107), channel_id=1, source_target_pairs={{28,0},{0,4},{4,8},{8,12},{12,16},{16,20},{20,24},{24,28},{29,1},{... | collective-permute-start | bytes 1572872 | tf_op jit(solution)/shard_map/while/body/eval_jaxpr/ppermute | solution.py:13
  492.2 32.1 %collective-permute-start.2 = (bf16[256,1024]{0,1:T(8,128)(2,1)}, bf16[256,1024]{0,1:T(8,128)(2,1)}, u32[]{:S(2)}, u32[]{:S(2)}) collective-permute-start(bf16[256,1024]{0,1:T(8,128)(2,1)} %fusion.170), channel_id=1, source_target_pairs={{28,0},{0,4},{4,8},{8,12},{12,16},{16,20},{20,24},{24,28},{29,1},{... | collective-permute-start | bytes 1572872 | tf_op jit(solution)/shard_map/while/body/eval_jaxpr/ppermute | solution.py:13
  495.5 37.4 %collective-permute-start.3 = (bf16[256,1024]{0,1:T(8,128)(2,1)}, bf16[256,1024]{0,1:T(8,128)(2,1)}, u32[]{:S(2)}, u32[]{:S(2)}) collective-permute-start(bf16[256,1024]{0,1:T(8,128)(2,1)} %fusion.172), channel_id=1, source_target_pairs={{28,0},{0,4},{4,8},{8,12},{12,16},{16,20},{20,24},{24,28},{29,1},{... | collective-permute-start | bytes 1572872 | tf_op jit(solution)/shard_map/while/body/eval_jaxpr/ppermute | solution.py:13
  498.5 36.5 %copy-start.21 = (bf16[256,1024]{0,1:T(8,128)(2,1)S(1)}, bf16[256,1024]{0,1:T(8,128)(2,1)}, u32[]{:S(2)}) copy-start(bf16[256,1024]{0,1:T(8,128)(2,1)} %copy-done.20) | copy-start | bytes 1572868 | tf_op jit(solution)/shard_map/while
  499.2 35.8 %copy-start.3 = (f32[256,1024]{0,1:T(8,128)}, f32[256,1024]{0,1:T(8,128)S(1)}, u32[]{:S(2)}) copy-start(f32[256,1024]{0,1:T(8,128)S(1)} %bitcast_add_fusion.4) | copy-start | bytes 3145732 | tf_op jit(solution)/shard_map/while
  536.3 50.0 %collective-permute-start = (bf16[256,1024]{0,1:T(8,128)(2,1)S(1)}, bf16[256,1024]{0,1:T(8,128)(2,1)}, u32[]{:S(2)}, u32[]{:S(2)}) collective-permute-start(bf16[256,1024]{0,1:T(8,128)(2,1)S(1)} %copy.106), channel_id=1, source_target_pairs={{28,0},{0,4},{4,8},{8,12},{12,16},{16,20},{20,24},{24,28},{29,1},{... | collective-permute-start | bytes 1572872 | tf_op jit(solution)/shard_map/while/body/eval_jaxpr/ppermute | solution.py:13
  538.2 48.1 %collective-permute-start.1 = (bf16[256,1024]{0,1:T(8,128)(2,1)}, bf16[256,1024]{0,1:T(8,128)(2,1)}, u32[]{:S(2)}, u32[]{:S(2)}) collective-permute-start(bf16[256,1024]{0,1:T(8,128)(2,1)} %copy.107), channel_id=1, source_target_pairs={{28,0},{0,4},{4,8},{8,12},{12,16},{16,20},{20,24},{24,28},{29,1},{... | collective-permute-start | bytes 1572872 | tf_op jit(solution)/shard_map/while/body/eval_jaxpr/ppermute | solution.py:13
  544.4 32.0 %collective-permute-start.2 = (bf16[256,1024]{0,1:T(8,128)(2,1)}, bf16[256,1024]{0,1:T(8,128)(2,1)}, u32[]{:S(2)}, u32[]{:S(2)}) collective-permute-start(bf16[256,1024]{0,1:T(8,128)(2,1)} %fusion.170), channel_id=1, source_target_pairs={{28,0},{0,4},{4,8},{8,12},{12,16},{16,20},{20,24},{24,28},{29,1},{... | collective-permute-start | bytes 1572872 | tf_op jit(solution)/shard_map/while/body/eval_jaxpr/ppermute | solution.py:13
  547.8 36.5 %collective-permute-start.3 = (bf16[256,1024]{0,1:T(8,128)(2,1)}, bf16[256,1024]{0,1:T(8,128)(2,1)}, u32[]{:S(2)}, u32[]{:S(2)}) collective-permute-start(bf16[256,1024]{0,1:T(8,128)(2,1)} %fusion.172), channel_id=1, source_target_pairs={{28,0},{0,4},{4,8},{8,12},{12,16},{16,20},{20,24},{24,28},{29,1},{... | collective-permute-start | bytes 1572872 | tf_op jit(solution)/shard_map/while/body/eval_jaxpr/ppermute | solution.py:13
  548.9 37.4 %copy-start.21 = (bf16[256,1024]{0,1:T(8,128)(2,1)S(1)}, bf16[256,1024]{0,1:T(8,128)(2,1)}, u32[]{:S(2)}) copy-start(bf16[256,1024]{0,1:T(8,128)(2,1)} %copy-done.20) | copy-start | bytes 1572868 | tf_op jit(solution)/shard_map/while
  549.6 36.7 %copy-start.3 = (f32[256,1024]{0,1:T(8,128)}, f32[256,1024]{0,1:T(8,128)S(1)}, u32[]{:S(2)}) copy-start(f32[256,1024]{0,1:T(8,128)S(1)} %bitcast_add_fusion.4) | copy-start | bytes 3145732 | tf_op jit(solution)/shard_map/while
  587.6 49.1 %collective-permute-start = (bf16[256,1024]{0,1:T(8,128)(2,1)S(1)}, bf16[256,1024]{0,1:T(8,128)(2,1)}, u32[]{:S(2)}, u32[]{:S(2)}) collective-permute-start(bf16[256,1024]{0,1:T(8,128)(2,1)S(1)} %copy.106), channel_id=1, source_target_pairs={{28,0},{0,4},{4,8},{8,12},{12,16},{16,20},{20,24},{24,28},{29,1},{... | collective-permute-start | bytes 1572872 | tf_op jit(solution)/shard_map/while/body/eval_jaxpr/ppermute | solution.py:13
  589.4 47.2 %collective-permute-start.1 = (bf16[256,1024]{0,1:T(8,128)(2,1)}, bf16[256,1024]{0,1:T(8,128)(2,1)}, u32[]{:S(2)}, u32[]{:S(2)}) collective-permute-start(bf16[256,1024]{0,1:T(8,128)(2,1)} %copy.107), channel_id=1, source_target_pairs={{28,0},{0,4},{4,8},{8,12},{12,16},{16,20},{20,24},{24,28},{29,1},{... | collective-permute-start | bytes 1572872 | tf_op jit(solution)/shard_map/while/body/eval_jaxpr/ppermute | solution.py:13
  595.7 32.0 %collective-permute-start.2 = (bf16[256,1024]{0,1:T(8,128)(2,1)}, bf16[256,1024]{0,1:T(8,128)(2,1)}, u32[]{:S(2)}, u32[]{:S(2)}) collective-permute-start(bf16[256,1024]{0,1:T(8,128)(2,1)} %fusion.170), channel_id=1, source_target_pairs={{28,0},{0,4},{4,8},{8,12},{12,16},{16,20},{20,24},{24,28},{29,1},{... | collective-permute-start | bytes 1572872 | tf_op jit(solution)/shard_map/while/body/eval_jaxpr/ppermute | solution.py:13
  599.0 35.5 %collective-permute-start.3 = (bf16[256,1024]{0,1:T(8,128)(2,1)}, bf16[256,1024]{0,1:T(8,128)(2,1)}, u32[]{:S(2)}, u32[]{:S(2)}) collective-permute-start(bf16[256,1024]{0,1:T(8,128)(2,1)} %fusion.172), channel_id=1, source_target_pairs={{28,0},{0,4},{4,8},{8,12},{12,16},{16,20},{20,24},{24,28},{29,1},{... | collective-permute-start | bytes 1572872 | tf_op jit(solution)/shard_map/while/body/eval_jaxpr/ppermute | solution.py:13
  599.8 36.9 %copy-start.21 = (bf16[256,1024]{0,1:T(8,128)(2,1)S(1)}, bf16[256,1024]{0,1:T(8,128)(2,1)}, u32[]{:S(2)}) copy-start(bf16[256,1024]{0,1:T(8,128)(2,1)} %copy-done.20) | copy-start | bytes 1572868 | tf_op jit(solution)/shard_map/while
  600.5 36.2 %copy-start.3 = (f32[256,1024]{0,1:T(8,128)}, f32[256,1024]{0,1:T(8,128)S(1)}, u32[]{:S(2)}) copy-start(f32[256,1024]{0,1:T(8,128)S(1)} %bitcast_add_fusion.4) | copy-start | bytes 3145732 | tf_op jit(solution)/shard_map/while
  637.9 48.1 %collective-permute-start = (bf16[256,1024]{0,1:T(8,128)(2,1)S(1)}, bf16[256,1024]{0,1:T(8,128)(2,1)}, u32[]{:S(2)}, u32[]{:S(2)}) collective-permute-start(bf16[256,1024]{0,1:T(8,128)(2,1)S(1)} %copy.106), channel_id=1, source_target_pairs={{28,0},{0,4},{4,8},{8,12},{12,16},{16,20},{20,24},{24,28},{29,1},{... | collective-permute-start | bytes 1572872 | tf_op jit(solution)/shard_map/while/body/eval_jaxpr/ppermute | solution.py:13
  639.8 46.3 %collective-permute-start.1 = (bf16[256,1024]{0,1:T(8,128)(2,1)}, bf16[256,1024]{0,1:T(8,128)(2,1)}, u32[]{:S(2)}, u32[]{:S(2)}) collective-permute-start(bf16[256,1024]{0,1:T(8,128)(2,1)} %copy.107), channel_id=1, source_target_pairs={{28,0},{0,4},{4,8},{8,12},{12,16},{16,20},{20,24},{24,28},{29,1},{... | collective-permute-start | bytes 1572872 | tf_op jit(solution)/shard_map/while/body/eval_jaxpr/ppermute | solution.py:13
  646.0 32.0 %collective-permute-start.2 = (bf16[256,1024]{0,1:T(8,128)(2,1)}, bf16[256,1024]{0,1:T(8,128)(2,1)}, u32[]{:S(2)}, u32[]{:S(2)}) collective-permute-start(bf16[256,1024]{0,1:T(8,128)(2,1)} %fusion.170), channel_id=1, source_target_pairs={{28,0},{0,4},{4,8},{8,12},{12,16},{16,20},{20,24},{24,28},{29,1},{... | collective-permute-start | bytes 1572872 | tf_op jit(solution)/shard_map/while/body/eval_jaxpr/ppermute | solution.py:13
  649.4 34.6 %collective-permute-start.3 = (bf16[256,1024]{0,1:T(8,128)(2,1)}, bf16[256,1024]{0,1:T(8,128)(2,1)}, u32[]{:S(2)}, u32[]{:S(2)}) collective-permute-start(bf16[256,1024]{0,1:T(8,128)(2,1)} %fusion.172), channel_id=1, source_target_pairs={{28,0},{0,4},{4,8},{8,12},{12,16},{16,20},{20,24},{24,28},{29,1},{... | collective-permute-start | bytes 1572872 | tf_op jit(solution)/shard_map/while/body/eval_jaxpr/ppermute | solution.py:13
  650.1 35.9 %copy-start.21 = (bf16[256,1024]{0,1:T(8,128)(2,1)S(1)}, bf16[256,1024]{0,1:T(8,128)(2,1)}, u32[]{:S(2)}) copy-start(bf16[256,1024]{0,1:T(8,128)(2,1)} %copy-done.20) | copy-start | bytes 1572868 | tf_op jit(solution)/shard_map/while
  650.8 35.3 %copy-start.3 = (f32[256,1024]{0,1:T(8,128)}, f32[256,1024]{0,1:T(8,128)S(1)}, u32[]{:S(2)}) copy-start(f32[256,1024]{0,1:T(8,128)S(1)} %bitcast_add_fusion.4) | copy-start | bytes 3145732 | tf_op jit(solution)/shard_map/while
  687.3 47.2 %collective-permute-start = (bf16[256,1024]{0,1:T(8,128)(2,1)S(1)}, bf16[256,1024]{0,1:T(8,128)(2,1)}, u32[]{:S(2)}, u32[]{:S(2)}) collective-permute-start(bf16[256,1024]{0,1:T(8,128)(2,1)S(1)} %copy.106), channel_id=1, source_target_pairs={{28,0},{0,4},{4,8},{8,12},{12,16},{16,20},{20,24},{24,28},{29,1},{... | collective-permute-start | bytes 1572872 | tf_op jit(solution)/shard_map/while/body/eval_jaxpr/ppermute | solution.py:13
  689.2 45.4 %collective-permute-start.1 = (bf16[256,1024]{0,1:T(8,128)(2,1)}, bf16[256,1024]{0,1:T(8,128)(2,1)}, u32[]{:S(2)}, u32[]{:S(2)}) collective-permute-start(bf16[256,1024]{0,1:T(8,128)(2,1)} %copy.107), channel_id=1, source_target_pairs={{28,0},{0,4},{4,8},{8,12},{12,16},{16,20},{20,24},{24,28},{29,1},{... | collective-permute-start | bytes 1572872 | tf_op jit(solution)/shard_map/while/body/eval_jaxpr/ppermute | solution.py:13
  695.5 31.4 %collective-permute-start.2 = (bf16[256,1024]{0,1:T(8,128)(2,1)}, bf16[256,1024]{0,1:T(8,128)(2,1)}, u32[]{:S(2)}, u32[]{:S(2)}) collective-permute-start(bf16[256,1024]{0,1:T(8,128)(2,1)} %fusion.170), channel_id=1, source_target_pairs={{28,0},{0,4},{4,8},{8,12},{12,16},{16,20},{20,24},{24,28},{29,1},{... | collective-permute-start | bytes 1572872 | tf_op jit(solution)/shard_map/while/body/eval_jaxpr/ppermute | solution.py:13
  698.8 33.7 %collective-permute-start.3 = (bf16[256,1024]{0,1:T(8,128)(2,1)}, bf16[256,1024]{0,1:T(8,128)(2,1)}, u32[]{:S(2)}, u32[]{:S(2)}) collective-permute-start(bf16[256,1024]{0,1:T(8,128)(2,1)} %fusion.172), channel_id=1, source_target_pairs={{28,0},{0,4},{4,8},{8,12},{12,16},{16,20},{20,24},{24,28},{29,1},{... | collective-permute-start | bytes 1572872 | tf_op jit(solution)/shard_map/while/body/eval_jaxpr/ppermute | solution.py:13
  699.6 35.0 %copy-start.21 = (bf16[256,1024]{0,1:T(8,128)(2,1)S(1)}, bf16[256,1024]{0,1:T(8,128)(2,1)}, u32[]{:S(2)}) copy-start(bf16[256,1024]{0,1:T(8,128)(2,1)} %copy-done.20) | copy-start | bytes 1572868 | tf_op jit(solution)/shard_map/while
  700.2 34.3 %copy-start.3 = (f32[256,1024]{0,1:T(8,128)}, f32[256,1024]{0,1:T(8,128)S(1)}, u32[]{:S(2)}) copy-start(f32[256,1024]{0,1:T(8,128)S(1)} %bitcast_add_fusion.4) | copy-start | bytes 3145732 | tf_op jit(solution)/shard_map/while
  735.9 46.3 %collective-permute-start = (bf16[256,1024]{0,1:T(8,128)(2,1)S(1)}, bf16[256,1024]{0,1:T(8,128)(2,1)}, u32[]{:S(2)}, u32[]{:S(2)}) collective-permute-start(bf16[256,1024]{0,1:T(8,128)(2,1)S(1)} %copy.106), channel_id=1, source_target_pairs={{28,0},{0,4},{4,8},{8,12},{12,16},{16,20},{20,24},{24,28},{29,1},{... | collective-permute-start | bytes 1572872 | tf_op jit(solution)/shard_map/while/body/eval_jaxpr/ppermute | solution.py:13
  737.7 44.4 %collective-permute-start.1 = (bf16[256,1024]{0,1:T(8,128)(2,1)}, bf16[256,1024]{0,1:T(8,128)(2,1)}, u32[]{:S(2)}, u32[]{:S(2)}) collective-permute-start(bf16[256,1024]{0,1:T(8,128)(2,1)} %copy.107), channel_id=1, source_target_pairs={{28,0},{0,4},{4,8},{8,12},{12,16},{16,20},{20,24},{24,28},{29,1},{... | collective-permute-start | bytes 1572872 | tf_op jit(solution)/shard_map/while/body/eval_jaxpr/ppermute | solution.py:13
  744.0 30.5 %collective-permute-start.2 = (bf16[256,1024]{0,1:T(8,128)(2,1)}, bf16[256,1024]{0,1:T(8,128)(2,1)}, u32[]{:S(2)}, u32[]{:S(2)}) collective-permute-start(bf16[256,1024]{0,1:T(8,128)(2,1)} %fusion.170), channel_id=1, source_target_pairs={{28,0},{0,4},{4,8},{8,12},{12,16},{16,20},{20,24},{24,28},{29,1},{... | collective-permute-start | bytes 1572872 | tf_op jit(solution)/shard_map/while/body/eval_jaxpr/ppermute | solution.py:13
  747.3 32.8 %collective-permute-start.3 = (bf16[256,1024]{0,1:T(8,128)(2,1)}, bf16[256,1024]{0,1:T(8,128)(2,1)}, u32[]{:S(2)}, u32[]{:S(2)}) collective-permute-start(bf16[256,1024]{0,1:T(8,128)(2,1)} %fusion.172), channel_id=1, source_target_pairs={{28,0},{0,4},{4,8},{8,12},{12,16},{16,20},{20,24},{24,28},{29,1},{... | collective-permute-start | bytes 1572872 | tf_op jit(solution)/shard_map/while/body/eval_jaxpr/ppermute | solution.py:13
  748.1 34.1 %copy-start.21 = (bf16[256,1024]{0,1:T(8,128)(2,1)S(1)}, bf16[256,1024]{0,1:T(8,128)(2,1)}, u32[]{:S(2)}) copy-start(bf16[256,1024]{0,1:T(8,128)(2,1)} %copy-done.20) | copy-start | bytes 1572868 | tf_op jit(solution)/shard_map/while
  785.7 68.3 %reduce-scatter.9.cloned.1.call-start = ((), (), s32[]{:S(2)}) async-start(), calls=%async_computation.14 | async-start | bytes 2621440 | tf_op jit(solution)/shard_map/reduce_scatter | solution.py:108
  787.9 95.1 %reduce-scatter.11.cloned.1.call-start = ((), (), s32[]{:S(2)}) async-start(), calls=%async_computation.15 | async-start | bytes 2621440 | tf_op jit(solution)/shard_map/reduce_scatter | solution.py:108
  791.1 166.1 %reduce-scatter.15.cloned.1.call-start = ((), (), s32[]{:S(2)}) async-start(), calls=%async_computation.17 | async-start | bytes 10485760 | tf_op jit(solution)/shard_map/reduce_scatter | solution.py:108
  798.6 233.1 %reduce-scatter.17.cloned.1.call-start = ((), (), s32[]{:S(2)}) async-start(), calls=%async_computation.18 | async-start | bytes 10485760 | tf_op jit(solution)/shard_map/reduce_scatter | solution.py:108
  (62 other events, 277.5 us)
Sparse Core Ops, SparseCore 0:
  9.6 25.2 all-gather.7
  36.5 22.5 all-gather.9
  60.7 22.5 all-gather.13
  85.8 124.9 all-gather.11
  212.2 20.7 all-gather.15
  234.4 58.2 all-gather.17
  294.3 58.2 all-gather.19
  375.6 31.4 reduce-scatter.12
  785.9 27.9 reduce-scatter.6
  816.2 32.5 reduce-scatter.8
  851.5 31.4 reduce-scatter.10
  885.4 71.6 reduce-scatter.14
  959.9 71.6 reduce-scatter.16
